TPU v7x, 32 devices: a whole 2x2x4 slice. The times are simulated.
32 devices in a mesh: groups: 2 (over x), rows: 8 (over z, y), cols: 2 (over core).
Axes of the slice: x: 2, y: 2, z: 4, core: 2. Of those that a mesh axis runs over, the one named last changes fastest.
Arguments:
- features: bfloat16 [80, 256, 1024], P(('groups', 'rows'), 'cols'), parts along dimension 0, may hold values from -6 to 6
- upstream: bfloat16 [80, 256, 1024], P(('groups', 'rows'), 'cols'), parts along dimension 0, may hold values from -6 to 6
- tile_valid: int32 [10, 32], P('groups'), parts along dimension 0, may hold values 0 or 1
- depthwise: bfloat16 [7, 7, 1024], replicated, may hold values from -0.875 to 0.875
- depthbias: float32 [1024], replicated, may hold values from -4 to 4
- norm_gain: float32 [1024], replicated, may hold values from 0.1 to 1.9
- norm_shift: float32 [1024], replicated, may hold values from -3 to 3
- expand: bfloat16 [1024, 2048], replicated, may hold values from -0.1875 to 0.1875
- expandbias: float32 [2048], replicated, may hold values from -3 to 3
- project: bfloat16 [2048, 1024], replicated, may hold values from -0.125 to 0.125
- projectbias: float32 [1024], replicated, may hold values from -4 to 4
- layer_scale: float32 [1024], replicated, may hold values from -4 to 4
Outputs:
- features_grad: bfloat16 [80, 256, 1024], P(('groups', 'rows'), 'cols'), parts along dimension 0
- depthwise_grad: float32 [14, 7, 1024], P('groups'), parts along dimension 0
- depthbias_grad: float32 [2048], P('groups'), parts along dimension 0
- gain_grad: float32 [2048], P('groups'), parts along dimension 0
- shift_grad: float32 [2048], P('groups'), parts along dimension 0
- expand_grad: float32 [2048, 2048], P(('groups', 'rows', 'cols')), parts along dimension 0
- expandbias_grad: float32 [4096], P('groups'), parts along dimension 0
- project_grad: float32 [4096, 1024], P(('groups', 'rows', 'cols')), parts along dimension 0
- projectbias_grad: float32 [2048], P('groups'), parts along dimension 0
- scale_grad: float32 [2048], P('groups'), parts along dimension 0
There are 2 independent parts, one for each index of `groups`. A program takes and returns all parts, laid end to end along the dimension named above; an argument that names none is the same for every part. Nothing has to cross between parts.
Inputs may be any that keep to these rules, and one draw needn't show every extreme that they name: `tile_valid`: 1 marks a tile of 8 x 8 cells with data.
All inputs are finite; a program needn't handle non-finite values.
Results may differ from a plain program's by a relative error of at most 0.0063.
Values may be sent and summed in bfloat16 or wider, within the bound.
A program may use at most 128 MiB of HBM per device.

v0:
```python
import jax
import jax.numpy as jnp
from jax import lax
from jax.experimental import pallas as pl
from jax.experimental.pallas import tpu as pltpu
from jax.sharding import PartitionSpec as P

MESH = pl.DeviceIdType.MESH
EDGE = 16
REACH = 3
TILE = 32
LANES = 128


class Halo:
    def __init__(self, own, pad, send, recv):
        height, breadth, _ = own.shape
        self.row, self.col = lax.axis_index("rows"), lax.axis_index("cols")
        self.rows = lax.axis_size("rows")
        self.own, self.pad = own, pad
        self.height, self.breadth = height, breadth
        row, other = self.row, 1 - self.col
        far = EDGE + breadth
        near = pl.ds(pl.multiple_of(other * (breadth - EDGE), EDGE), EDGE)
        there = pl.ds(pl.multiple_of(self.col * far, EDGE), EDGE)
        here = pl.ds(pl.multiple_of(other * far, EDGE), EDGE)
        mid = pl.ds(EDGE, breadth)
        full = pl.ds(0, breadth)
        top, bottom = pl.ds(0, REACH), pl.ds(REACH + height, REACH)
        first, last = pl.ds(0, REACH), pl.ds(height - REACH, REACH)
        inner, every = pl.ds(REACH, height), pl.ds(0, height)

        def pair(k, source, target, landing, device):
            def copy(spot):
                return pltpu.make_async_remote_copy(
                    src_ref=own.at[source[0], source[1]],
                    dst_ref=pad.at[spot[0], spot[1]],
                    send_sem=send.at[k],
                    recv_sem=recv.at[k],
                    device_id=device,
                    device_id_type=MESH,
                )

            return copy(target), copy(landing)

        up, down = ({"rows": row - 1}, {"rows": row + 1})
        self.edge = pair(0, (every, near), (inner, there), (inner, here), {"cols": other})
        self.to_next = (
            pair(1, (last, full), (top, mid), (top, mid), down),
            pair(3, (last, near), (top, there), (top, here), {**down, "cols": other}),
        )
        self.to_previous = (
            pair(2, (first, full), (bottom, mid), (bottom, mid), up),
            pair(4, (first, near), (bottom, there), (bottom, here), {**up, "cols": other}),
        )

    def start(self):
        row, rows, col = self.row, self.rows, self.col
        barrier = pltpu.get_barrier_semaphore()

        def greet(device):
            pl.semaphore_signal(barrier, inc=1, device_id=device, device_id_type=MESH)

        greet({"cols": 1 - col})

        @pl.when(row > 0)
        def _():
            greet({"rows": row - 1})
            greet({"rows": row - 1, "cols": 1 - col})

        @pl.when(row < rows - 1)
        def _():
            greet({"rows": row + 1})
            greet({"rows": row + 1, "cols": 1 - col})

        pl.semaphore_wait(
            barrier, 1 + 2 * (row > 0).astype(jnp.int32) + 2 * (row < rows - 1).astype(jnp.int32)
        )

        @pl.when(row < rows - 1)
        def _():
            for out, _ in self.to_next:
                out.start()

        @pl.when(row > 0)
        def _():
            for out, _ in self.to_previous:
                out.start()

        self.edge[0].start()
        pad, height, far = self.pad, self.height, EDGE + self.breadth

        def clear(rows_at, cols_at):
            shape = (rows_at.stop - rows_at.start, cols_at.stop - cols_at.start, pad.shape[2])
            pad[rows_at, cols_at, :] = jnp.zeros(shape, pad.dtype)

        @pl.when(col == 0)
        def _():
            clear(slice(0, pad.shape[0]), slice(0, EDGE))

        @pl.when(col == 1)
        def _():
            clear(slice(0, pad.shape[0]), slice(far, far + EDGE))

        for at_end, rows_at in (
            (row == 0, slice(0, REACH)),
            (row == rows - 1, slice(REACH + height, 2 * REACH + height)),
        ):

            @pl.when(at_end & (col == 0))
            def _():
                clear(rows_at, slice(EDGE, far + EDGE))

            @pl.when(at_end & (col == 1))
            def _():
                clear(rows_at, slice(0, far))

        pad[REACH : REACH + height, EDGE:far, :] = self.own[...]

    def wait_edge(self):
        self.edge[1].wait_recv()

    def wait_rows(self):
        @pl.when(self.row > 0)
        def _():
            for _, landed in self.to_next:
                landed.wait_recv()

        @pl.when(self.row < self.rows - 1)
        def _():
            for _, landed in self.to_previous:
                landed.wait_recv()

    def finish(self):
        self.edge[0].wait_send()

        @pl.when(self.row < self.rows - 1)
        def _():
            for out, _ in self.to_next:
                out.wait_send()

        @pl.when(self.row > 0)
        def _():
            for out, _ in self.to_previous:
                out.wait_send()


def over_lanes(width, body):
    def step(index, carry):
        body(pl.ds(pl.multiple_of(index * LANES, LANES), LANES))
        return carry

    lax.fori_loop(0, width // LANES, step, 0)


def conv_rows(pad, stage, weight, base, total, in_rows, finish):
    height, breadth, width = total.shape

    def chunk(lanes):
        for i in in_rows:
            stage[i] = pad[i, :, lanes].astype(jnp.float32)

        def tile(t, carry):
            start = pl.multiple_of(t * TILE, TILE)
            cells = pl.ds(start, TILE)
            sums = [base(r, cells, lanes) for r in range(height)]
            for b in range(7):
                for i in in_rows:
                    window = stage[i, pl.ds(start + EDGE - REACH + b, TILE), :]
                    for r in range(height):
                        if 0 <= i - r < 7:
                            tap = weight[pl.ds((i - r) * 7 + b, 1), lanes]
                            sums[r] = sums[r] + window * tap
            for r in range(height):
                total[r, cells, lanes] = finish(sums[r])
            return carry

        lax.fori_loop(0, breadth // TILE, tile, 0)

    over_lanes(width, chunk)


def sum_taps(pad, stage, grad, parts, out):
    height, breadth, width = grad.shape

    def chunk(lanes):
        for i in range(height + 2 * REACH):
            stage[i] = pad[i, :, lanes].astype(jnp.float32)
        parts[...] = jnp.zeros_like(parts)

        def tile(t, carry):
            start = pl.multiple_of(t * TILE, TILE)
            near = [
                grad[r, pl.ds(start, TILE), lanes].astype(jnp.float32) for r in range(height)
            ]
            for b in range(7):
                sums = [None] * 7
                for i in range(height + 2 * REACH):
                    window = stage[i, pl.ds(start + EDGE - REACH + b, TILE), :]
                    for r in range(height):
                        a = i - r
                        if 0 <= a < 7:
                            term = window * near[r]
                            sums[a] = term if sums[a] is None else sums[a] + term
                for a in range(7):
                    parts[7 * a + b] += jnp.sum(sums[a].reshape(TILE // 8, 8, LANES), axis=0)
            return carry

        lax.fori_loop(0, breadth // TILE, tile, 0)
        out[:, lanes] = jnp.sum(parts[...], axis=1)

    over_lanes(width, chunk)


def forward_kernel(own, weight, bias, mixed, pad_out, pad, stage, send, recv):
    height, _, _ = own.shape
    halo = Halo(own, pad, send, recv)
    halo.start()
    halo.wait_edge()
    same = lambda value: value
    start = lambda r, cells, lanes: jnp.broadcast_to(bias[:, lanes], (TILE, LANES))
    conv_rows(pad, stage, weight, start, mixed, range(REACH, REACH + height), same)
    halo.wait_rows()
    border = [*range(REACH), *range(REACH + height, 2 * REACH + height)]
    conv_rows(pad, stage, weight, lambda r, cells, lanes: mixed[r, cells, lanes], mixed, border, same)
    pad_out[...] = pad[...]
    halo.finish()


def backward_kernel(
    own, weight, masked, features, grad, taps, pad, stage, total, parts, send, recv
):
    height, _, _ = own.shape
    halo = Halo(own, pad, send, recv)
    halo.start()
    sum_taps(features, stage, own, parts, taps)
    halo.wait_edge()
    start = lambda r, cells, lanes: masked[r, cells, lanes]
    conv_rows(pad, stage, weight, start, total, range(REACH, REACH + height), lambda value: value)
    halo.wait_rows()
    border = [*range(REACH), *range(REACH + height, 2 * REACH + height)]
    start = lambda r, cells, lanes: total[r, cells, lanes]
    conv_rows(pad, stage, weight, start, grad, border, lambda value: value.astype(grad.dtype))
    halo.finish()


def halo_call(kernel, shape, outs, extra, ident, passes):
    height, breadth, width = shape
    vmem = pl.BlockSpec(memory_space=pltpu.VMEM)
    padded = (height + 2 * REACH, breadth + 2 * EDGE)
    flops = 98 * height * breadth * width * passes
    return pl.pallas_call(
        kernel,
        out_shape=outs,
        in_specs=[vmem] * (3 if ident == 0 else 4),
        out_specs=[vmem] * len(outs),
        scratch_shapes=[
            pltpu.VMEM((*padded, width), jnp.bfloat16),
            pltpu.VMEM((*padded, LANES), jnp.float32),
            *extra,
            pltpu.SemaphoreType.DMA((5,)),
            pltpu.SemaphoreType.DMA((5,)),
        ],
        compiler_params=pltpu.CompilerParams(
            collective_id=ident, has_side_effects=True, vmem_limit_bytes=48 * 1024 * 1024
        ),
        cost_estimate=pl.CostEstimate(flops=flops, bytes_accessed=8 * 1024 * 1024, transcendentals=0),
    )


def split_rows(row_count):
    low = 1
    while low * low * 4 <= row_count:
        low *= 2
    return row_count // low, low


def stage(value, axis, dim, size, place, perm_of):
    total = lax.dynamic_index_in_dim(value, place, dim, keepdims=False)
    for step in range(1, size):
        theirs = lax.dynamic_index_in_dim(value, (place + step) % size, dim, keepdims=False)
        got = lax.ppermute(theirs.astype(jnp.bfloat16), axis, perm_of(step))
        total = total + got.astype(jnp.float32)
    return total


def scatter_sum(partial):
    rows, cols = (lax.axis_size("rows"), lax.axis_size("cols"))
    high, low = split_rows(rows)
    row, col = (lax.axis_index("rows"), lax.axis_index("cols"))
    block = partial.shape[0] // (rows * cols)
    value = partial.reshape(high, low, cols, block, partial.shape[1])
    value = stage(
        value, "cols", 2, cols, col, lambda k: [(i, (i + k) % cols) for i in range(cols)]
    )
    value = stage(
        value,
        "rows",
        1,
        low,
        row % low,
        lambda k: [(i, i // low * low + (i % low + k) % low) for i in range(rows)],
    )
    return stage(
        value, "rows", 0, high, row // low, lambda k: [(i, (i + k * low) % rows) for i in range(rows)]
    )


def whole_sum(value):
    for axis in ("cols", "rows"):
        size = lax.axis_size(axis)
        bit = 1
        while bit < size:
            value = value + lax.ppermute(value, axis, [(i, i ^ bit) for i in range(size)])
            bit *= 2
    return value


def per_device(
    features,
    upstream,
    tile_valid,
    depthwise,
    depthbias,
    norm_gain,
    norm_shift,
    expand,
    expandbias,
    project,
    projectbias,
    layer_scale,
):
    height, breadth, width = features.shape
    row_count = lax.axis_size("rows")
    col_count = lax.axis_size("cols")
    taps = depthwise.astype(jnp.float32).reshape(49, width)
    padded_shape = (height + 2 * REACH, breadth + 2 * EDGE, width)
    mixed, padded = halo_call(
        forward_kernel,
        features.shape,
        [
            jax.ShapeDtypeStruct(features.shape, jnp.float32),
            jax.ShapeDtypeStruct(padded_shape, jnp.bfloat16),
        ],
        [],
        0,
        1,
    )(features, taps, depthbias[None])
    centred = mixed - jnp.mean(mixed, axis=-1, keepdims=True)
    rstd = lax.rsqrt(jnp.mean(centred * centred, axis=-1, keepdims=True) + 1e-06)
    normed_f = centred * rstd
    normed = (normed_f * norm_gain + norm_shift).astype(jnp.bfloat16).reshape(-1, width)
    pre = jnp.dot(normed, expand, preferred_element_type=jnp.float32) + expandbias
    cdf = 0.5 * (1.0 + lax.erf(pre * 0.7071067811865476))
    act = (pre * cdf).astype(jnp.bfloat16)
    out_branch = jnp.dot(act, project, preferred_element_type=jnp.float32) + projectbias
    row_cells = lax.axis_index("rows") * height + jnp.arange(height, dtype=jnp.int32)
    col_cells = lax.axis_index("cols") * breadth + jnp.arange(breadth, dtype=jnp.int32)
    row_pick = (
        row_cells[:, None] // 8 == jnp.arange(tile_valid.shape[0], dtype=jnp.int32)[None, :]
    ).astype(jnp.float32)
    col_pick = (
        col_cells[:, None] // 8 == jnp.arange(tile_valid.shape[1], dtype=jnp.int32)[None, :]
    ).astype(jnp.float32)
    row_tiles = jnp.dot(row_pick, tile_valid.astype(jnp.float32), precision=lax.Precision.HIGHEST)
    cells = lax.dot_general(
        row_tiles, col_pick, (((1,), (1,)), ((), ())), precision=lax.Precision.HIGHEST
    )
    masked = (upstream.astype(jnp.float32) * cells[:, :, None]).reshape(-1, width)
    branch_grad = (masked * layer_scale).astype(jnp.bfloat16)
    act_grad = lax.dot_general(
        branch_grad, project, (((1,), (1,)), ((), ())), preferred_element_type=jnp.float32
    )
    slope = cdf + pre * jnp.exp(-0.5 * pre * pre) * 0.3989422804014327
    pre_grad = (act_grad * slope).astype(jnp.bfloat16)
    normed_grad = lax.dot_general(
        pre_grad, expand, (((1,), (1,)), ((), ())), preferred_element_type=jnp.float32
    ).reshape(height, breadth, width)
    gained = normed_grad * norm_gain
    mixed_grad = (
        rstd
        * (
            gained
            - jnp.mean(gained, axis=-1, keepdims=True)
            - normed_f * jnp.mean(gained * normed_f, axis=-1, keepdims=True)
        )
    ).astype(jnp.bfloat16)
    features_grad, tap_sums = halo_call(
        backward_kernel,
        features.shape,
        [
            jax.ShapeDtypeStruct(features.shape, jnp.bfloat16),
            jax.ShapeDtypeStruct((49, width), jnp.float32),
        ],
        [
            pltpu.VMEM(features.shape, jnp.float32),
            pltpu.VMEM((49, 8, LANES), jnp.float32),
        ],
        1,
        2,
    )(mixed_grad, taps[::-1], masked.reshape(height, breadth, width), padded)
    factor = float(height * row_count * breadth * col_count) ** (-0.5)
    expand_grad = scatter_sum(
        lax.dot_general(
            normed, pre_grad, (((0,), (0,)), ((), ())), preferred_element_type=jnp.float32
        )
        * factor
    )
    project_grad = scatter_sum(
        lax.dot_general(
            act, branch_grad, (((0,), (0,)), ((), ())), preferred_element_type=jnp.float32
        )
        * factor
    )
    grad_f = mixed_grad.astype(jnp.float32)
    local_sums = (
        tap_sums,
        jnp.sum(grad_f, axis=(0, 1)),
        jnp.sum(normed_grad * normed_f, axis=(0, 1)),
        jnp.sum(normed_grad, axis=(0, 1)),
        jnp.sum(pre_grad.astype(jnp.float32), axis=0),
        jnp.sum(branch_grad.astype(jnp.float32), axis=0),
        jnp.sum(masked * out_branch, axis=0),
    )
    packed = jnp.concatenate([value.reshape(-1, width) for value in local_sums], axis=0)
    packed = whole_sum(packed) * factor
    hidden = expand.shape[1]
    depthwise_grad = packed[:49].reshape(7, 7, width)
    depthbias_grad = packed[49]
    gain_grad = packed[50]
    shift_grad = packed[51]
    expandbias_grad = packed[52 : 52 + hidden // width].reshape(hidden)
    projectbias_grad = packed[52 + hidden // width]
    scale_grad = packed[53 + hidden // width]
    return (
        features_grad,
        depthwise_grad,
        depthbias_grad,
        gain_grad,
        shift_grad,
        expand_grad,
        expandbias_grad,
        project_grad,
        projectbias_grad,
        scale_grad,
    )


def solution(mesh):
    return jax.shard_map(
        per_device,
        mesh=mesh,
        in_specs=(
            P(("groups", "rows"), "cols", None),
            P(("groups", "rows"), "cols", None),
            P("groups", None),
            P(),
            P(),
            P(),
            P(),
            P(),
            P(),
            P(),
            P(),
            P(),
        ),
        out_specs=(
            P(("groups", "rows"), "cols", None),
            P("groups", None, None),
            P("groups"),
            P("groups"),
            P("groups"),
            P(("groups", "rows", "cols"), None),
            P("groups"),
            P(("groups", "rows", "cols"), None),
            P("groups"),
            P("groups"),
        ),
        check_vma=False,
    )
```

profile of v0, /device:TPU:0, one launch (start us, length us, event | category | flops | bytes accessed | tf_op | source)
XLA Modules:
  0.0 254.2 jit_solution(15682225662430178779)
XLA Ops:
  0.7 0.9 reshape.200.weight
  1.6 0.0 copy-start.2
  1.6 1.3 copy-done.2
  2.9 0.7 copy-done.3
  3.6 43.3 %shard_map.195 = (f32[5,128,1024]{2,1,0:T(8,128)S(1)}, bf16[11,160,1024]{2,1,0:T(8,128)(2,1)}) custom-call(bf16[5,128,1024]{2,1,0:T(8,128)(2,1)S(1)} %copy-done.2, f32[49,1024]{1,0:T(8,128)S(1)} %reshape.200.weight, f32[1,1024]{1,0:T(1,128)S(1)} %bitcast.83), custom_call_target="tpu_custom_call" | custom-call | flops 64225280 | bytes 8388608 | tf_op jit(solution)/shard_map/pallas_call | solution.py:338
  46.9 0.2 reduce_sum.90
  47.2 0.4 multiply_reduce_fusion.3
  47.6 0.0 copy-done.17
  47.6 0.2 fusion.24
  47.8 0.2 fusion.22
  48.0 1.8 convert_reduce_fusion.1
  49.9 1.5 copy-done
  51.3 0.3 fusion.6
  51.7 0.5 add_convert_fusion
  52.2 1.8 copy-done.13
  54.0 4.7 %multiply_convert_fusion = (bf16[640,2048]{1,0:T(8,128)(2,1)}, f32[640,2048]{1,0:T(8,128)S(1)}) fusion(f32[2048]{0:T(1024)S(1)} %copy-done.16, bf16[640,1024]{1,0:T(8,128)(2,1)S(1)} %bitcast.88, bf16[1024,2048]{1,0:T(8,128)(2,1)S(1)} %copy-done.13), kind=kOutput, calls=%fused_computation.7 | convolution fusion | flops 2692218880 | bytes 13377536 | tf_op jit(solution)/shard_map/dot_general | solution.py:353
  58.7 5.1 %convert_reduce_fusion = (f32[2048]{0:T(1024)S(1)}, bf16[640,2048]{1,0:T(8,128)(2,1)S(1)}) fusion(f32[640,2048]{1,0:T(8,128)S(1)} %get-tuple-element.41, f32[2048]{0:T(1024)S(1)} %copy-done.16, bf16[640,1024]{1,0:T(8,128)(2,1)S(1)} %fusion.6, bf16[2048,1024]{1,0:T(8,128)(2,1)S(1)} %copy-done.15), kind=kOutput, calls=%fused_computation.8 | convolution fusion | flops 2701391872 | bytes 13385728 | tf_op jit(solution)/shard_map/dot_general | solution.py:371
  63.9 1.5 copy-done.19
  65.3 5.6 %convolution_multiply_fusion.1 = f32[1024,2048]{1,0:T(8,128)} fusion(bf16[640,1024]{1,0:T(8,128)(2,1)S(1)} %bitcast.89, bf16[640,2048]{1,0:T(8,128)(2,1)S(1)} %get-tuple-element.39), kind=kOutput, calls=%fused_computation.11 | convolution fusion | flops 2686451712 | bytes 12320768 | tf_op jit(solution)/shard_map/dot_general | solution.py:404
  71.0 4.0 %fusion.8 = bf16[4,2,64,2048]{3,2,0,1:T(8,128)(2,1)} fusion(f32[4,2,2,64,2048]{4,3,2,1,0:T(8,128)} %bitcast.86, s32[]{:T(128)S(6)} %select_n.106), kind=kLoop, calls=%fused_computation.31 | loop fusion | bytes 4194308 | tf_op jit(solution)/shard_map/convert_element_type | solution.py:282
  75.0 5.7 %convolution_multiply_fusion = f32[2048,1024]{1,0:T(8,128)} fusion(bf16[640,2048]{1,0:T(8,128)(2,1)S(1)} %copy-done.21, bf16[640,1024]{1,0:T(8,128)(2,1)S(1)} %copy-done.8), kind=kOutput, calls=%fused_computation.10 | convolution fusion | flops 2686451712 | bytes 12320768 | tf_op jit(solution)/shard_map/dot_general | solution.py:410
  80.7 4.0 %fusion.9 = bf16[4,2,128,1024]{3,2,0,1:T(8,128)(2,1)} fusion(f32[4,2,2,128,1024]{4,3,2,1,0:T(8,128)} %bitcast.22, s32[]{:T(128)S(6)} %select_n.106), kind=kLoop, calls=%fused_computation.32 | loop fusion | bytes 4194308 | tf_op jit(solution)/shard_map/convert_element_type | solution.py:282
  84.6 0.5 collective-permute-start.9
  85.1 4.4 %fusion.27 = (f32[1024]{0:T(1024)S(1)}, f32[640]{0:T(1024)S(1)}, f32[640,1024]{1,0:T(8,128)}) fusion(f32[1024]{0:T(1024)S(1)} %copy-done.10, bf16[640,2048]{1,0:T(8,128)(2,1)S(1)} %copy-done.20, bf16[1024,2048]{1,0:T(8,128)(2,1)S(1)} %copy-done.14), kind=kOutput, calls=%fused_computation.83 | convolution fusion | flops 2686319104 | bytes 9447936 | tf_op jit(solution)/shard_map/dot_general | solution.py:376
  89.5 0.4 rev.3.weight
  90.0 2.5 multiply_reduce_fusion
  92.6 6.8 %fusion.7 = f32[1024]{0:T(1024)S(1)} fusion(f32[5,128,1024]{2,1,0:T(8,128)} %copy-done, bf16[640,2048]{1,0:T(8,128)(2,1)} %get-tuple-element.40, bf16[2048,1024]{1,0:T(8,128)(2,1)} %param.21, f32[1024]{0:T(1024)S(1)} %copy-done.18), kind=kOutput, calls=%fused_computation.19 | convolution fusion | flops 2686319616 | bytes 9445376 | tf_op jit(solution)/shard_map/dot_general | solution.py:356
  99.4 0.9 convert_reduce_fusion.2
  100.3 0.8 copy-done.1
  101.1 47.4 %shard_map.196 = (bf16[5,128,1024]{2,1,0:T(8,128)(2,1)S(1)}, f32[49,1024]{1,0:T(8,128)S(1)}) custom-call(bf16[5,128,1024]{2,1,0:T(8,128)(2,1)S(1)} %get-tuple-element.23.own, f32[49,1024]{1,0:T(8,128)S(1)} %rev.3.weight, f32[5,128,1024]{2,1,0:T(8,128)S(1)} %copy-done.1, bf16[11,160,1024]{2,1,0:T(8,128)(2,1)} %get-tuple-element.15.features), custom_call_target="tpu_custom_call" | custom-call | flops 128450560 | bytes 8388608 | tf_op jit(solution)/shard_map/pallas_call | solution.py:388
  148.5 0.1 concatenate.3
  148.6 0.1 collective-permute-start
  148.7 1.5 collective-permute-done
  150.2 6.6 %collective-permute-start.1 = (f32[56,1024]{1,0:T(8,128)S(1)}, f32[56,1024]{1,0:T(8,128)S(1)}, u32[]{:S(2)}, u32[]{:S(2)}) collective-permute-start(f32[56,1024]{1,0:T(8,128)S(1)} %add.217), channel_id=1, source_target_pairs={{0,2},{2,0},{4,6},{6,4},{8,10},{10,8},{12,14},{14,12},{1,3},{3,1},... | collective-permute-start | bytes 688136 | tf_op jit(solution)/shard_map/ppermute | solution.py:314
  156.8 6.1 %collective-permute-done.1 = f32[56,1024]{1,0:T(8,128)S(1)} collective-permute-done((f32[56,1024]{1,0:T(8,128)S(1)}, f32[56,1024]{1,0:T(8,128)S(1)}, u32[]{:S(2)}, u32[]{:S(2)}) %collective-permute-start.1) | collective-permute-done | bytes 229408 | tf_op jit(solution)/shard_map/ppermute | solution.py:314
  162.9 4.3 %collective-permute-start.2 = (f32[56,1024]{1,0:T(8,128)S(1)}, f32[56,1024]{1,0:T(8,128)S(1)}, u32[]{:S(2)}, u32[]{:S(2)}) collective-permute-start(f32[56,1024]{1,0:T(8,128)S(1)} %add.218), channel_id=1, source_target_pairs={{0,4},{2,6},{4,0},{6,2},{8,12},{10,14},{12,8},{14,10},{1,5},{3,7},... | collective-permute-start | bytes 688136 | tf_op jit(solution)/shard_map/ppermute | solution.py:314
  167.3 5.1 %collective-permute-done.2 = f32[56,1024]{1,0:T(8,128)S(1)} collective-permute-done((f32[56,1024]{1,0:T(8,128)S(1)}, f32[56,1024]{1,0:T(8,128)S(1)}, u32[]{:S(2)}, u32[]{:S(2)}) %collective-permute-start.2) | collective-permute-done | bytes 229408 | tf_op jit(solution)/shard_map/ppermute | solution.py:314
  172.4 1.8 collective-permute-start.3
  174.2 5.7 %bitcast_add_fusion.1 = f32[4,2,64,2048]{3,2,0,1:T(8,128)} fusion(bf16[4,2,64,2048]{3,2,0,1:T(8,128)(2,1)} %collective-permute-done.4, f32[4,2,2,64,2048]{4,3,2,1,0:T(8,128)} %bitcast.87, s32[]{:T(128)S(6)} %select_n.104), kind=kLoop, calls=%fused_computation.15 | loop fusion | flops 2097152 | bytes 10485764 | tf_op jit(solution)/shard_map/add | solution.py:283
  179.9 1.7 fusion.10
  181.6 0.3 collective-permute-start.5
  181.9 2.5 %collective-permute-done.3 = f32[56,1024]{1,0:T(8,128)S(1)} collective-permute-done((f32[56,1024]{1,0:T(8,128)S(1)}, f32[56,1024]{1,0:T(8,128)S(1)}, u32[]{:S(2)}, u32[]{:S(2)}) %collective-permute-start.3) | collective-permute-done | bytes 229408 | tf_op jit(solution)/shard_map/ppermute | solution.py:314
  184.5 3.6 %bitcast_add_fusion = f32[4,2,128,1024]{3,2,0,1:T(8,128)S(1)} fusion(bf16[4,2,128,1024]{3,2,0,1:T(8,128)(2,1)} %collective-permute-done.9, f32[4,2,2,128,1024]{4,3,2,1,0:T(8,128)} %bitcast.22, s32[]{:T(128)S(6)} %select_n.104), kind=kLoop, calls=%fused_computation.14 | loop fusion | flops 2097152 | bytes 10485764 | tf_op jit(solution)/shard_map/add | solution.py:283
  188.1 2.0 copy-done.4
  190.1 0.1 fusion.11
  190.2 1.0 collective-permute-start.10
  191.3 1.7 reshape.195
  192.9 0.6 copy.38
  193.5 1.6 fusion.28
  195.2 12.7 %collective-permute-done.5 = bf16[4,64,2048]{2,1,0:T(8,128)(2,1)} collective-permute-done((bf16[4,64,2048]{2,1,0:T(8,128)(2,1)S(1)}, bf16[4,64,2048]{2,1,0:T(8,128)(2,1)}, u32[]{:S(2)}, u32[]{:S(2)}) %collective-permute-start.5) | collective-permute-done | bytes 1048608 | tf_op jit(solution)/shard_map/ppermute | solution.py:282
  207.9 2.2 bitcast_add_fusion.3
  210.1 0.1 fusion.16
  210.2 2.4 collective-permute-start.8
  212.6 0.8 collective-permute-start.6
  213.4 14.2 %collective-permute-done.10 = bf16[4,128,1024]{2,1,0:T(8,128)(2,1)} collective-permute-done((bf16[4,128,1024]{2,1,0:T(8,128)(2,1)S(1)}, bf16[4,128,1024]{2,1,0:T(8,128)(2,1)}, u32[]{:S(2)}, u32[]{:S(2)}) %collective-permute-start.10) | collective-permute-done | bytes 1048608 | tf_op jit(solution)/shard_map/ppermute | solution.py:282
  227.6 1.7 bitcast_add_fusion.2
  229.3 0.1 fusion.19
  229.4 2.2 collective-permute-start.13
  231.6 1.1 collective-permute-start.11
  232.8 0.9 fusion.15
  233.7 4.7 %collective-permute-done.13 = bf16[128,1024]{1,0:T(8,128)(2,1)S(1)} collective-permute-done((bf16[128,1024]{1,0:T(8,128)(2,1)S(1)}, bf16[128,1024]{1,0:T(8,128)(2,1)S(1)}, u32[]{:S(2)}, u32[]{:S(2)}) %collective-permute-start.13) | collective-permute-done | bytes 262176 | tf_op jit(solution)/shard_map/ppermute | solution.py:282
  238.4 13.9 %collective-permute-done.12 = bf16[128,1024]{1,0:T(8,128)(2,1)S(1)} collective-permute-done((bf16[128,1024]{1,0:T(8,128)(2,1)S(1)}, bf16[128,1024]{1,0:T(8,128)(2,1)S(1)}, u32[]{:S(2)}, u32[]{:S(2)}) %collective-permute-start.12) | collective-permute-done | bytes 262176 | tf_op jit(solution)/shard_map/ppermute | solution.py:282
  252.2 0.9 fusion.13
  253.2 1.1 copy.40
  (56 shorter events, 0.3 us)
Async XLA Ops:
  1.6 1.3 copy-start.2
  2.9 0.7 copy-start.3
  46.9 0.7 copy-start.17
  46.9 1.1 copy-start.11
  49.8 1.5 copy-start
  49.8 1.8 copy-start.10
  49.8 1.8 copy-start.12
  51.3 2.7 %copy-start.13 = (bf16[1024,2048]{1,0:T(8,128)(2,1)S(1)}, bf16[1024,2048]{1,0:T(8,128)(2,1)}, u32[]{:S(2)}) copy-start(bf16[1024,2048]{1,0:T(8,128)(2,1)} %param.19) | copy-start | bytes 12582916
  51.7 7.0 %copy-start.7 = (bf16[640,1024]{1,0:T(8,128)(2,1)}, bf16[640,1024]{1,0:T(8,128)(2,1)S(1)}, u32[]{:S(2)}) copy-start(bf16[640,1024]{1,0:T(8,128)(2,1)S(1)} %fusion.6) | copy-start | bytes 3932164
  51.7 2.3 copy-start.16
  54.0 4.7 %copy-start.15 = (bf16[2048,1024]{1,0:T(8,128)(2,1)S(1)}, bf16[2048,1024]{1,0:T(8,128)(2,1)}, u32[]{:S(2)}) copy-start(bf16[2048,1024]{1,0:T(8,128)(2,1)} %param.21) | copy-start | bytes 12582916
  63.8 1.5 copy-start.19
  71.0 4.0 %copy-start.8 = (bf16[640,1024]{1,0:T(8,128)(2,1)S(1)}, bf16[640,1024]{1,0:T(8,128)(2,1)}, u32[]{:S(2)}) copy-start(bf16[640,1024]{1,0:T(8,128)(2,1)} %copy-done.7) | copy-start | bytes 3932164
  71.0 4.0 %copy-start.21 = (bf16[640,2048]{1,0:T(8,128)(2,1)S(1)}, bf16[640,2048]{1,0:T(8,128)(2,1)}, u32[]{:S(2)}) copy-start(bf16[640,2048]{1,0:T(8,128)(2,1)} %get-tuple-element.40) | copy-start | bytes 7864324
  74.9 99.3 %collective-permute-start.4 = (bf16[4,2,64,2048]{3,2,0,1:T(8,128)(2,1)}, bf16[4,2,64,2048]{3,2,0,1:T(8,128)(2,1)}, u32[]{:S(2)}, u32[]{:S(2)}) collective-permute-start(bf16[4,2,64,2048]{3,2,0,1:T(8,128)(2,1)} %fusion.8), channel_id=1, source_target_pairs={{0,1},{1,0},{2,3},{3,2},{4,5},{5,4},{6,7},{7,6},{8,9},{9,8},{10,11... | collective-permute-start | bytes 6291464 | tf_op jit(solution)/shard_map/ppermute | solution.py:282
  75.0 10.2 %copy-start.20 = (bf16[640,2048]{1,0:T(8,128)(2,1)S(1)}, bf16[640,2048]{1,0:T(8,128)(2,1)}, u32[]{:S(2)}) copy-start(bf16[640,2048]{1,0:T(8,128)(2,1)} %copy-done.19) | copy-start | bytes 7864324
  80.7 4.5 %copy-start.14 = (bf16[1024,2048]{1,0:T(8,128)(2,1)S(1)}, bf16[1024,2048]{1,0:T(8,128)(2,1)}, u32[]{:S(2)}) copy-start(bf16[1024,2048]{1,0:T(8,128)(2,1)} %param.19) | copy-start | bytes 12582916
  84.6 99.8 %collective-permute-start.9 = (bf16[4,2,128,1024]{3,2,0,1:T(8,128)(2,1)}, bf16[4,2,128,1024]{3,2,0,1:T(8,128)(2,1)}, u32[]{:S(2)}, u32[]{:S(2)}) collective-permute-start(bf16[4,2,128,1024]{3,2,0,1:T(8,128)(2,1)} %fusion.9), channel_id=1, source_target_pairs={{0,1},{1,0},{2,3},{3,2},{4,5},{5,4},{6,7},{7,6},{8,9},{9,8},{10,11... | collective-permute-start | bytes 6291464 | tf_op jit(solution)/shard_map/ppermute | solution.py:282
  90.0 2.6 %copy-start.18 = (f32[1024]{0:T(1024)S(1)}, f32[1024]{0:T(1024)}, u32[]{:S(2)}) copy-start(f32[1024]{0:T(1024)} %param.22) | copy-start | bytes 12292
  92.6 6.8 %copy-start.6 = (f32[640,1024]{1,0:T(8,128)S(1)}, f32[640,1024]{1,0:T(8,128)}, u32[]{:S(2)}) copy-start(f32[640,1024]{1,0:T(8,128)} %get-tuple-element.37) | copy-start | bytes 7864324
  99.4 1.7 copy-start.1
  148.6 1.6 collective-permute-start
  150.2 12.7 %collective-permute-start.1 = (f32[56,1024]{1,0:T(8,128)S(1)}, f32[56,1024]{1,0:T(8,128)S(1)}, u32[]{:S(2)}, u32[]{:S(2)}) collective-permute-start(f32[56,1024]{1,0:T(8,128)S(1)} %add.217), channel_id=1, source_target_pairs={{0,2},{2,0},{4,6},{6,4},{8,10},{10,8},{12,14},{14,12},{1,3},{3,1},... | collective-permute-start | bytes 688136 | tf_op jit(solution)/shard_map/ppermute | solution.py:314
  162.9 9.4 %collective-permute-start.2 = (f32[56,1024]{1,0:T(8,128)S(1)}, f32[56,1024]{1,0:T(8,128)S(1)}, u32[]{:S(2)}, u32[]{:S(2)}) collective-permute-start(f32[56,1024]{1,0:T(8,128)S(1)} %add.218), channel_id=1, source_target_pairs={{0,4},{2,6},{4,0},{6,2},{8,12},{10,14},{12,8},{14,10},{1,5},{3,7},... | collective-permute-start | bytes 688136 | tf_op jit(solution)/shard_map/ppermute | solution.py:314
  172.4 12.1 %collective-permute-start.3 = (f32[56,1024]{1,0:T(8,128)S(1)}, f32[56,1024]{1,0:T(8,128)S(1)}, u32[]{:S(2)}, u32[]{:S(2)}) collective-permute-start(f32[56,1024]{1,0:T(8,128)S(1)} %add.219), channel_id=1, source_target_pairs={{0,8},{2,10},{4,12},{6,14},{8,0},{10,2},{12,4},{14,6},{1,9},{3,11}... | collective-permute-start | bytes 688136 | tf_op jit(solution)/shard_map/ppermute | solution.py:314
  181.6 26.3 %collective-permute-start.5 = (bf16[4,64,2048]{2,1,0:T(8,128)(2,1)S(1)}, bf16[4,64,2048]{2,1,0:T(8,128)(2,1)}, u32[]{:S(2)}, u32[]{:S(2)}) collective-permute-start(bf16[4,64,2048]{2,1,0:T(8,128)(2,1)S(1)} %fusion.10), channel_id=1, source_target_pairs={{0,2},{2,0},{4,6},{6,4},{8,10},{10,8},{12,14},{14,12},{1,3},{3,1},... | collective-permute-start | bytes 3145736 | tf_op jit(solution)/shard_map/ppermute | solution.py:282
  184.5 6.8 %copy-start.9 = (f32[56,1024]{1,0:T(8,128)}, f32[56,1024]{1,0:T(8,128)S(1)}, u32[]{:S(2)}) copy-start(f32[56,1024]{1,0:T(8,128)S(1)} %add_multiply_fusion.1) | copy-start | bytes 688132
  188.1 2.0 copy-start.4
  190.2 37.4 %collective-permute-start.10 = (bf16[4,128,1024]{2,1,0:T(8,128)(2,1)S(1)}, bf16[4,128,1024]{2,1,0:T(8,128)(2,1)}, u32[]{:S(2)}, u32[]{:S(2)}) collective-permute-start(bf16[4,128,1024]{2,1,0:T(8,128)(2,1)S(1)} %fusion.11), channel_id=1, source_target_pairs={{0,2},{2,0},{4,6},{6,4},{8,10},{10,8},{12,14},{14,12},{1,3},{3,1},... | collective-permute-start | bytes 3145736 | tf_op jit(solution)/shard_map/ppermute | solution.py:282
  195.2 32.5 %copy-start.5 = (f32[4,2,128,1024]{3,2,0,1:T(8,128)S(1)}, f32[4,2,128,1024]{3,2,0,1:T(8,128)}, u32[]{:S(2)}) copy-start(f32[4,2,128,1024]{3,2,0,1:T(8,128)} %copy-done.4) | copy-start | bytes 12582916
  210.2 21.4 %collective-permute-start.8 = (bf16[64,2048]{1,0:T(8,128)(2,1)S(1)}, bf16[64,2048]{1,0:T(8,128)(2,1)S(1)}, u32[]{:S(2)}, u32[]{:S(2)}) collective-permute-start(bf16[64,2048]{1,0:T(8,128)(2,1)S(1)} %get-tuple-element.28), channel_id=1, source_target_pairs={{0,12},{2,14},{4,0},{6,2},{8,4},{10,6},{12,8},{14,10},{1,13},{3,15... | collective-permute-start | bytes 786440 | tf_op jit(solution)/shard_map/ppermute | solution.py:282
  212.6 20.2 %collective-permute-start.7 = (bf16[64,2048]{1,0:T(8,128)(2,1)S(1)}, bf16[64,2048]{1,0:T(8,128)(2,1)S(1)}, u32[]{:S(2)}, u32[]{:S(2)}) collective-permute-start(bf16[64,2048]{1,0:T(8,128)(2,1)S(1)} %get-tuple-element.29), channel_id=1, source_target_pairs={{0,8},{2,10},{4,12},{6,14},{8,0},{10,2},{12,4},{14,6},{1,9},{3,11}... | collective-permute-start | bytes 786440 | tf_op jit(solution)/shard_map/ppermute | solution.py:282
  212.6 20.2 %collective-permute-start.6 = (bf16[64,2048]{1,0:T(8,128)(2,1)S(1)}, bf16[64,2048]{1,0:T(8,128)(2,1)S(1)}, u32[]{:S(2)}, u32[]{:S(2)}) collective-permute-start(bf16[64,2048]{1,0:T(8,128)(2,1)S(1)} %get-tuple-element.27), channel_id=1, source_target_pairs={{0,4},{2,6},{4,8},{6,10},{8,12},{10,14},{12,0},{14,2},{1,5},{3,7},... | collective-permute-start | bytes 786440 | tf_op jit(solution)/shard_map/ppermute | solution.py:282
  229.4 9.0 %collective-permute-start.13 = (bf16[128,1024]{1,0:T(8,128)(2,1)S(1)}, bf16[128,1024]{1,0:T(8,128)(2,1)S(1)}, u32[]{:S(2)}, u32[]{:S(2)}) collective-permute-start(bf16[128,1024]{1,0:T(8,128)(2,1)S(1)} %get-tuple-element.25), channel_id=1, source_target_pairs={{0,12},{2,14},{4,0},{6,2},{8,4},{10,6},{12,8},{14,10},{1,13},{3,15... | collective-permute-start | bytes 786440 | tf_op jit(solution)/shard_map/ppermute | solution.py:282
  231.6 20.6 %collective-permute-start.12 = (bf16[128,1024]{1,0:T(8,128)(2,1)S(1)}, bf16[128,1024]{1,0:T(8,128)(2,1)S(1)}, u32[]{:S(2)}, u32[]{:S(2)}) collective-permute-start(bf16[128,1024]{1,0:T(8,128)(2,1)S(1)} %get-tuple-element.26), channel_id=1, source_target_pairs={{0,8},{2,10},{4,12},{6,14},{8,0},{10,2},{12,4},{14,6},{1,9},{3,11}... | collective-permute-start | bytes 786440 | tf_op jit(solution)/shard_map/ppermute | solution.py:282
  231.6 20.6 %collective-permute-start.11 = (bf16[128,1024]{1,0:T(8,128)(2,1)S(1)}, bf16[128,1024]{1,0:T(8,128)(2,1)S(1)}, u32[]{:S(2)}, u32[]{:S(2)}) collective-permute-start(bf16[128,1024]{1,0:T(8,128)(2,1)S(1)} %get-tuple-element.24), channel_id=1, source_target_pairs={{0,4},{2,6},{4,8},{6,10},{8,12},{10,14},{12,0},{14,2},{1,5},{3,7},... | collective-permute-start | bytes 786440 | tf_op jit(solution)/shard_map/ppermute | solution.py:282
where the time goes:
time: 255 us; the launch traced here: 254 us
  Pallas kernels  90.7 us (36%)
  waiting for transfers between devices  60.7 us (24%)
  matrix products  32.7 us (13%)
  local copies, waits for them, and re-layouts  26 us (10%)
  other arithmetic  21.8 us (9%)
  starting transfers between devices  21.3 us (8%)
    pallas_call x1, Pallas kernels, per_device(): halo_call(backward_kernel, features.shape, [jax.ShapeDtypeStruct(features...  47.4 us
    ppermute x10, waiting for transfers between devices, stage(): got = lax.ppermute(theirs.astype(jnp.bfloat16), axis, perm_of(step))  45.5 us
    pallas_call x1, Pallas kernels, per_device(): halo_call(forward_kernel, features.shape, [jax.ShapeDtypeStruct(features....  43.3 us
    ppermute x4, waiting for transfers between devices, whole_sum(): lax.ppermute(value, axis, [(i, i ^ bit) for i in range(size)])  15.2 us
    add x6, other arithmetic, stage(): total = total + got.astype(jnp.float32)  14.9 us
    ppermute x4, starting transfers between devices, whole_sum(): lax.ppermute(value, axis, [(i, i ^ bit) for i in range(size)])  12.9 us
    unnamed x47, local copies, waits for them, and re-layouts  11.2 us
    convert_element_type x6, local copies, waits for them, and re-layouts, stage(): got = lax.ppermute(theirs.astype(jnp.bfloat16), axis, perm_of(step))  10.1 us
  transfers between devices with their start and end apart: 14, of which 8 were waited for; matrix products, arithmetic and copies ran while one was open for 18% of the time, Pallas kernels for 19%

commit v1 on v0

--- a/solution.py
+++ b/solution.py
@@ -275,35 +275,49 @@
     return row_count // low, low
 
 
-def stage(value, axis, dim, size, place, perm_of):
-    total = lax.dynamic_index_in_dim(value, place, dim, keepdims=False)
-    for step in range(1, size):
-        theirs = lax.dynamic_index_in_dim(value, (place + step) % size, dim, keepdims=False)
-        got = lax.ppermute(theirs.astype(jnp.bfloat16), axis, perm_of(step))
-        total = total + got.astype(jnp.float32)
-    return total
-
-
-def scatter_sum(partial):
+def pick(value, dim, size, place):
+    own = lax.dynamic_index_in_dim(value, place, dim, keepdims=False)
+    theirs = [
+        lax.dynamic_index_in_dim(value, (place + step) % size, dim, keepdims=False).astype(
+            jnp.bfloat16
+        )
+        for step in range(1, size)
+    ]
+    return own, theirs
+
+
+def exchange(own, theirs, axis, perm_of):
+    for step, part in enumerate(theirs, 1):
+        own = own + lax.ppermute(part, axis, perm_of(step)).astype(jnp.float32)
+    return own
+
+
+def over_cores(partial):
     rows, cols = (lax.axis_size("rows"), lax.axis_size("cols"))
     high, low = split_rows(rows)
-    row, col = (lax.axis_index("rows"), lax.axis_index("cols"))
     block = partial.shape[0] // (rows * cols)
     value = partial.reshape(high, low, cols, block, partial.shape[1])
-    value = stage(
-        value, "cols", 2, cols, col, lambda k: [(i, (i + k) % cols) for i in range(cols)]
-    )
-    value = stage(
-        value,
+    own, theirs = pick(value, 2, cols, lax.axis_index("cols"))
+    value = exchange(own, theirs, "cols", lambda k: [(i, (i + k) % cols) for i in range(cols)])
+    return pick(value, 1, low, lax.axis_index("rows") % low)
+
+
+def over_low(own, theirs):
+    rows = lax.axis_size("rows")
+    high, low = split_rows(rows)
+    value = exchange(
+        own,
+        theirs,
         "rows",
-        1,
-        low,
-        row % low,
         lambda k: [(i, i // low * low + (i % low + k) % low) for i in range(rows)],
     )
-    return stage(
-        value, "rows", 0, high, row // low, lambda k: [(i, (i + k * low) % rows) for i in range(rows)]
-    )
+    return pick(value, 0, high, lax.axis_index("rows") // low)
+
+
+def over_high(own, theirs):
+    rows = lax.axis_size("rows")
+    _, low = split_rows(rows)
+    return exchange(own, theirs, "rows", lambda k: [(i, (i + k * low) % rows) for i in range(rows)])
 
 
 def whole_sum(value):
@@ -385,6 +399,22 @@
             - normed_f * jnp.mean(gained * normed_f, axis=-1, keepdims=True)
         )
     ).astype(jnp.bfloat16)
+    factor = float(height * row_count * breadth * col_count) ** (-0.5)
+    project_low, project_sent = over_cores(
+        lax.dot_general(
+            act, branch_grad, (((0,), (0,)), ((), ())), preferred_element_type=jnp.float32
+        )
+        * factor
+    )
+    expand_low, expand_sent = over_cores(
+        lax.dot_general(
+            normed, pre_grad, (((0,), (0,)), ((), ())), preferred_element_type=jnp.float32
+        )
+        * factor
+    )
+    mixed_grad, project_sent, expand_sent = lax.optimization_barrier(
+        (mixed_grad, project_sent, expand_sent)
+    )
     features_grad, tap_sums = halo_call(
         backward_kernel,
         features.shape,
@@ -399,19 +429,6 @@
         1,
         2,
     )(mixed_grad, taps[::-1], masked.reshape(height, breadth, width), padded)
-    factor = float(height * row_count * breadth * col_count) ** (-0.5)
-    expand_grad = scatter_sum(
-        lax.dot_general(
-            normed, pre_grad, (((0,), (0,)), ((), ())), preferred_element_type=jnp.float32
-        )
-        * factor
-    )
-    project_grad = scatter_sum(
-        lax.dot_general(
-            act, branch_grad, (((0,), (0,)), ((), ())), preferred_element_type=jnp.float32
-        )
-        * factor
-    )
     grad_f = mixed_grad.astype(jnp.float32)
     local_sums = (
         tap_sums,
@@ -423,7 +440,14 @@
         jnp.sum(masked * out_branch, axis=0),
     )
     packed = jnp.concatenate([value.reshape(-1, width) for value in local_sums], axis=0)
+    project_high, project_sent = over_low(project_low, project_sent)
+    expand_high, expand_sent = over_low(expand_low, expand_sent)
+    packed, project_sent, expand_sent = lax.optimization_barrier(
+        (packed, project_sent, expand_sent)
+    )
     packed = whole_sum(packed) * factor
+    project_grad = over_high(project_high, project_sent)
+    expand_grad = over_high(expand_high, expand_sent)
     hidden = expand.shape[1]
     depthwise_grad = packed[:49].reshape(7, 7, width)
     depthbias_grad = packed[49]

time: 255 us -> 269 us (1.055)
  waiting for transfers between devices: 60.7 us -> 27.9 us
  Pallas kernels: 90.7 us -> 122 us
  starting transfers between devices: 21.3 us -> 40 us
  matrix products: 32.7 us -> 27.4 us
    ppermute x10, waiting for transfers between devices: 45.5 us -> 6.77 us  [exchange(): own = own + lax.ppermute(part, axis, perm_of(step)).astype(jnp.float32)]
    pallas_call x1, Pallas kernels: 47.4 us -> 78.9 us  [per_device(): halo_call(backward_kernel, features.shape, [jax.ShapeDtypeStruct(features...]
    ppermute x10, starting transfers between devices: 8.38 us -> 21.4 us  [exchange(): own = own + lax.ppermute(part, axis, perm_of(step)).astype(jnp.float32)]
    ppermute x4, waiting for transfers between devices: 15.2 us -> 21.1 us  [whole_sum(): lax.ppermute(value, axis, [(i, i ^ bit) for i in range(size)])]
    ppermute x4, starting transfers between devices: 12.9 us -> 18.6 us  [whole_sum(): lax.ppermute(value, axis, [(i, i ^ bit) for i in range(size)])]
    dot_general x1, matrix products: 6.78 us -> 2.92 us  [per_device(): jnp.dot(act, project, preferred_element_type=jnp.float32) + projectbias]
    unnamed x47 -> x65, local copies, waits for them, and re-layouts: 11.2 us -> 14.8 us
  transfers between devices with their start and end apart: 14 -> 14, of which waited for: 8 -> 4; matrix products, arithmetic and copies ran while one was open for 18% -> 11% of each run, Pallas kernels for 19% -> 29%
where the time goes in v1:
time: 269 us; the launch traced here: 268 us
  Pallas kernels  122 us (45%)
  starting transfers between devices  40 us (15%)
  waiting for transfers between devices  27.9 us (10%)
  matrix products  27.4 us (10%)
  local copies, waits for them, and re-layouts  25.7 us (10%)
  other arithmetic  23.8 us (9%)
    pallas_call x1, Pallas kernels, per_device(): halo_call(backward_kernel, features.shape, [jax.ShapeDtypeStruct(features...  78.9 us
    pallas_call x1, Pallas kernels, per_device(): halo_call(forward_kernel, features.shape, [jax.ShapeDtypeStruct(features....  43.3 us
    ppermute x10, starting transfers between devices, exchange(): own = own + lax.ppermute(part, axis, perm_of(step)).astype(jnp.float32)  21.4 us
    ppermute x4, waiting for transfers between devices, whole_sum(): lax.ppermute(value, axis, [(i, i ^ bit) for i in range(size)])  21.1 us
    ppermute x4, starting transfers between devices, whole_sum(): lax.ppermute(value, axis, [(i, i ^ bit) for i in range(size)])  18.6 us
    unnamed x65, local copies, waits for them, and re-layouts  14.8 us
    add x6, other arithmetic, exchange(): own = own + lax.ppermute(part, axis, perm_of(step)).astype(jnp.float32)  14.7 us
    convert_element_type x6, local copies, waits for them, and re-layouts, pick(): lax.dynamic_index_in_dim(value, (place + step) % size, dim, keepdims=False)  8.31 us
  transfers between devices with their start and end apart: 14, of which 4 were waited for; matrix products, arithmetic and copies ran while one was open for 11% of the time, Pallas kernels for 29%

profile of v1, /device:TPU:0, one launch (start us, length us, event | category | flops | bytes accessed | tf_op | source)
XLA Modules:
  0.0 268.3 jit_solution(789863685107210305)
XLA Ops:
  0.6 0.0 copy-start.17
  0.7 0.9 reshape.200.weight
  1.6 0.9 fusion.24
  2.5 0.2 fusion.22
  2.7 1.8 convert_reduce_fusion.1
  4.6 1.4 fusion.6
  6.0 0.5 copy-done
  6.5 0.4 copy-done.3
  6.9 43.3 %shard_map.195 = (f32[5,128,1024]{2,1,0:T(8,128)S(1)}, bf16[11,160,1024]{2,1,0:T(8,128)(2,1)}) custom-call(bf16[5,128,1024]{2,1,0:T(8,128)(2,1)S(1)} %copy-done.3, f32[49,1024]{1,0:T(8,128)S(1)} %reshape.200.weight, f32[1,1024]{1,0:T(1,128)S(1)} %bitcast.83), custom_call_target="tpu_custom_call" | custom-call | flops 64225280 | bytes 8388608 | tf_op jit(solution)/shard_map/pallas_call | solution.py:352
  50.2 0.2 reduce_sum.90
  50.4 0.4 multiply_reduce_fusion.3
  50.8 0.0 copy-done.16
  50.8 0.0 copy-done.18
  50.8 0.5 add_convert_fusion
  51.3 1.2 copy-done.19
  52.6 4.7 %multiply_convert_fusion = (bf16[640,2048]{1,0:T(8,128)(2,1)}, f32[640,2048]{1,0:T(8,128)S(1)}) fusion(f32[2048]{0:T(1024)S(1)} %copy-done.23, bf16[640,1024]{1,0:T(8,128)(2,1)S(1)} %bitcast.92, bf16[1024,2048]{1,0:T(8,128)(2,1)S(1)} %copy-done.19), kind=kOutput, calls=%fused_computation.8 | convolution fusion | flops 2692218880 | bytes 13377536 | tf_op jit(solution)/shard_map/dot_general | solution.py:367
  57.3 5.1 %convert_reduce_fusion = (f32[2048]{0:T(1024)S(1)}, bf16[640,2048]{1,0:T(8,128)(2,1)S(1)}) fusion(f32[640,2048]{1,0:T(8,128)S(1)} %get-tuple-element.57, f32[2048]{0:T(1024)S(1)} %copy-done.23, bf16[640,1024]{1,0:T(8,128)(2,1)S(1)} %copy-done.14, bf16[2048,1024]{1,0:T(8,128)(2,1)S(1)} %copy-done.21), kind=kOutput, calls=%fused_computation.7 | convolution fusion | flops 2701391872 | bytes 13385728 | tf_op jit(solution)/shard_map/dot_general | solution.py:385
  62.5 1.5 copy-done.25
  63.9 5.7 %convolution_multiply_fusion = f32[1024,2048]{1,0:T(8,128)} fusion(bf16[640,1024]{1,0:T(8,128)(2,1)S(1)} %bitcast.93, bf16[640,2048]{1,0:T(8,128)(2,1)S(1)} %get-tuple-element.59), kind=kOutput, calls=%fused_computation.10 | convolution fusion | flops 2686451712 | bytes 12320768 | tf_op jit(solution)/shard_map/dot_general | solution.py:410
  69.6 4.0 %fusion.9 = bf16[4,2,64,2048]{3,2,0,1:T(8,128)(2,1)} fusion(f32[4,2,2,64,2048]{4,3,2,1,0:T(8,128)} %bitcast.86, s32[]{:T(128)S(6)} %select_n.106), kind=kLoop, calls=%fused_computation.32 | loop fusion | bytes 4194308 | tf_op jit(solution)/shard_map/convert_element_type | solution.py:281
  73.6 3.5 %convolution_multiply_fusion.1 = f32[2048,1024]{1,0:T(8,128)S(1)} fusion(bf16[640,2048]{1,0:T(8,128)(2,1)S(1)} %copy-done.27, bf16[640,1024]{1,0:T(8,128)(2,1)S(1)} %copy-done.15), kind=kOutput, calls=%fused_computation.11 | convolution fusion | flops 2686451712 | bytes 12320768 | tf_op jit(solution)/shard_map/dot_general | solution.py:404
  77.1 4.2 %copy-done.13 = f32[2048,1024]{1,0:T(8,128)} copy-done((f32[2048,1024]{1,0:T(8,128)}, f32[2048,1024]{1,0:T(8,128)S(1)}, u32[]{:S(2)}) %copy-start.13) | copy-done | bytes 8388632
  81.3 1.6 fusion.8
  83.0 0.5 collective-permute-start
  83.5 4.4 %fusion.27 = (f32[1024]{0:T(1024)S(1)}, f32[640]{0:T(1024)S(1)}, f32[640,1024]{1,0:T(8,128)}) fusion(f32[1024]{0:T(1024)S(1)} %copy-done.16, bf16[640,2048]{1,0:T(8,128)(2,1)S(1)} %copy-done.26, bf16[1024,2048]{1,0:T(8,128)(2,1)S(1)} %copy-done.20), kind=kOutput, calls=%fused_computation.83 | convolution fusion | flops 2686319104 | bytes 9447936 | tf_op jit(solution)/shard_map/dot_general | solution.py:390
  87.9 2.7 %multiply_reduce_fusion = (f32[1024]{0:T(1024)S(1)}, f32[5,128]{1,0:T(8,128)S(1)}) fusion(f32[5,128,1024]{2,1,0:T(8,128)} %bitcast.84, f32[5,128,1024]{2,1,0:T(8,128)S(1)} %get-tuple-element.24, f32[5,128]{1,0:T(8,128)S(1)} %add_rsqrt_fusion, f32[5,128]{1,0:T(8,128)S(1)} %broadcast_multiply_fusion.1, f32[1024]{0:T(1024)S(1)} %copy-done.16), kind=kLoop, calls=%fused_computation.22 | loop fusion | flops 4585856 | bytes 5258752 | tf_op jit(solution)/shard_map/reduce_sum | solution.py:436
  90.6 1.8 multiply_convert_fusion.2.own
  92.4 3.6 %bitcast_add_fusion = f32[4,2,64,2048]{3,2,0,1:T(8,128)S(1)} fusion(bf16[4,2,64,2048]{3,2,0,1:T(8,128)(2,1)} %collective-permute-done.1, f32[4,2,2,64,2048]{4,3,2,1,0:T(8,128)} %bitcast.87, s32[]{:T(128)S(6)} %select_n.104), kind=kLoop, calls=%fused_computation.14 | loop fusion | flops 2097152 | bytes 10485764 | tf_op jit(solution)/shard_map/add | solution.py:291
  96.0 1.3 fusion.11
  97.4 3.1 %bitcast_add_fusion.1 = f32[4,2,128,1024]{3,2,0,1:T(8,128)S(1)} fusion(bf16[4,2,128,1024]{3,2,0,1:T(8,128)(2,1)} %collective-permute-done, f32[4,2,2,128,1024]{4,3,2,1,0:T(8,128)S(1)} %bitcast.91, s32[]{:T(128)S(6)} %select_n.104), kind=kLoop, calls=%fused_computation.15 | loop fusion | flops 2097152 | bytes 10485764 | tf_op jit(solution)/shard_map/add | solution.py:291
  100.5 1.1 fusion.10
  101.6 1.3 copy-done.9
  102.9 6.8 %collective-permute-start.2 = (bf16[4,128,1024]{2,1,0:T(8,128)(2,1)}, bf16[4,128,1024]{2,1,0:T(8,128)(2,1)}, u32[]{:S(2)}, u32[]{:S(2)}) collective-permute-start(bf16[4,128,1024]{2,1,0:T(8,128)(2,1)} %fusion.10), channel_id=1, source_target_pairs={{0,2},{2,0},{4,6},{6,4},{8,10},{10,8},{12,14},{14,12},{1,3},{3,1},... | collective-permute-start | bytes 3145736 | tf_op jit(solution)/shard_map/ppermute | solution.py:291
  109.7 0.0 collective-permute-start.3
  109.8 2.9 %fusion.7 = f32[1024]{0:T(1024)S(1)} fusion(f32[5,128,1024]{2,1,0:T(8,128)S(1)} %copy-done.1, bf16[640,2048]{1,0:T(8,128)(2,1)S(1)} %copy-done.28, bf16[2048,1024]{1,0:T(8,128)(2,1)S(1)} %copy-done.22, f32[1024]{0:T(1024)S(1)} %copy-done.24), kind=kOutput, calls=%fused_computation.19 | convolution fusion | flops 2686319616 | bytes 9445376 | tf_op jit(solution)/shard_map/dot_general | solution.py:370
  112.8 0.3 rev.3.weight
  113.1 1.3 copy-done.2
  114.4 78.9 %shard_map.196 = (bf16[5,128,1024]{2,1,0:T(8,128)(2,1)S(1)}, f32[49,1024]{1,0:T(8,128)S(1)}) custom-call(bf16[5,128,1024]{2,1,0:T(8,128)(2,1)S(1)} %copy-done.2, f32[49,1024]{1,0:T(8,128)S(1)} %rev.3.weight, f32[5,128,1024]{2,1,0:T(8,128)S(1)} %copy-done.1, bf16[11,160,1024]{2,1,0:T(8,128)(2,1)} %get-tuple-element.26.features), custom_call_target="tpu_custom_call" | custom-call | flops 128450560 | bytes 8388608 | tf_op jit(solution)/shard_map/pallas_call | solution.py:418
  193.3 0.2 convert_reduce_fusion.2
  193.6 0.8 copy-done.4
  194.4 0.1 concatenate.3
  194.5 2.4 bitcast_add_fusion.3
  196.9 0.1 fusion.18
  197.0 0.6 copy-done.8
  197.6 1.6 bitcast_add_fusion.2
  199.2 0.1 fusion.21
  199.3 1.2 copy-done.12
  200.5 8.1 %collective-permute-start.8 = (bf16[64,2048]{1,0:T(8,128)(2,1)S(1)}, bf16[64,2048]{1,0:T(8,128)(2,1)S(1)}, u32[]{:S(2)}, u32[]{:S(2)}) collective-permute-start(bf16[64,2048]{1,0:T(8,128)(2,1)S(1)} %get-tuple-element.32), channel_id=1, source_target_pairs={{0,4},{2,6},{4,8},{6,10},{8,12},{10,14},{12,0},{14,2},{1,5},{3,7},... | collective-permute-start | bytes 786440 | tf_op jit(solution)/shard_map/ppermute | solution.py:291
  208.6 1.4 collective-permute-start.9
  210.0 2.5 collective-permute-start.10
  212.5 0.5 collective-permute-start.5
  213.0 6.3 %collective-permute-done.5 = f32[56,1024]{1,0:T(8,128)S(1)} collective-permute-done((f32[56,1024]{1,0:T(8,128)S(1)}, f32[56,1024]{1,0:T(8,128)S(1)}, u32[]{:S(2)}, u32[]{:S(2)}) %collective-permute-start.5) | collective-permute-done | bytes 229408 | tf_op jit(solution)/shard_map/ppermute | solution.py:328
  219.3 2.0 collective-permute-start.13
  221.3 6.8 %collective-permute-done.9 = bf16[64,2048]{1,0:T(8,128)(2,1)} collective-permute-done((bf16[64,2048]{1,0:T(8,128)(2,1)S(1)}, bf16[64,2048]{1,0:T(8,128)(2,1)}, u32[]{:S(2)}, u32[]{:S(2)}) %collective-permute-start.9) | collective-permute-done | bytes 262176 | tf_op jit(solution)/shard_map/ppermute | solution.py:291
  228.1 16.4 %collective-permute-start.6 = (f32[56,1024]{1,0:T(8,128)S(1)}, f32[56,1024]{1,0:T(8,128)S(1)}, u32[]{:S(2)}, u32[]{:S(2)}) collective-permute-start(f32[56,1024]{1,0:T(8,128)S(1)} %add.240), channel_id=1, source_target_pairs={{0,4},{2,6},{4,0},{6,2},{8,12},{10,14},{12,8},{14,10},{1,5},{3,7},... | collective-permute-start | bytes 688136 | tf_op jit(solution)/shard_map/ppermute | solution.py:328
  244.4 2.1 fusion.15
  246.5 5.7 %collective-permute-done.6 = f32[56,1024]{1,0:T(8,128)S(1)} collective-permute-done((f32[56,1024]{1,0:T(8,128)S(1)}, f32[56,1024]{1,0:T(8,128)S(1)}, u32[]{:S(2)}, u32[]{:S(2)}) %collective-permute-start.6) | collective-permute-done | bytes 229408 | tf_op jit(solution)/shard_map/ppermute | solution.py:328
  252.2 1.8 collective-permute-start.7
  254.1 2.0 fusion.13
  256.1 9.2 %collective-permute-done.7 = f32[56,1024]{1,0:T(8,128)S(1)} collective-permute-done((f32[56,1024]{1,0:T(8,128)S(1)}, f32[56,1024]{1,0:T(8,128)S(1)}, u32[]{:S(2)}, u32[]{:S(2)}) %collective-permute-start.7) | collective-permute-done | bytes 229408 | tf_op jit(solution)/shard_map/ppermute | solution.py:328
  265.3 0.6 fusion.28
  265.9 0.6 copy.38
  266.5 0.7 reshape.197
  267.2 1.1 copy.40
  (76 shorter events, 0.3 us)
Async XLA Ops:
  0.6 3.9 %copy-start.17 = (f32[1024]{0:T(1024)S(1)}, f32[1024]{0:T(1024)}, u32[]{:S(2)}) copy-start(f32[1024]{0:T(1024)} %param.23) | copy-start | bytes 12292
  4.5 1.9 copy-start
  4.6 2.3 copy-start.3
  4.6 2.3 copy-start.6
  50.1 0.7 copy-start.16
  50.2 0.7 copy-start.18
  50.4 2.2 copy-start.19
  50.8 1.8 copy-start.23
  52.6 4.7 %copy-start.14 = (bf16[640,1024]{1,0:T(8,128)(2,1)S(1)}, bf16[640,1024]{1,0:T(8,128)(2,1)}, u32[]{:S(2)}) copy-start(bf16[640,1024]{1,0:T(8,128)(2,1)} %fusion.6) | copy-start | bytes 3932164
  52.6 4.7 %copy-start.21 = (bf16[2048,1024]{1,0:T(8,128)(2,1)S(1)}, bf16[2048,1024]{1,0:T(8,128)(2,1)}, u32[]{:S(2)}) copy-start(bf16[2048,1024]{1,0:T(8,128)(2,1)} %param.21) | copy-start | bytes 12582916
  62.5 1.5 copy-start.25
  69.6 4.0 %copy-start.15 = (bf16[640,1024]{1,0:T(8,128)(2,1)S(1)}, bf16[640,1024]{1,0:T(8,128)(2,1)}, u32[]{:S(2)}) copy-start(bf16[640,1024]{1,0:T(8,128)(2,1)} %fusion.6) | copy-start | bytes 3932164
  69.6 4.0 %copy-start.27 = (bf16[640,2048]{1,0:T(8,128)(2,1)S(1)}, bf16[640,2048]{1,0:T(8,128)(2,1)}, u32[]{:S(2)}) copy-start(bf16[640,2048]{1,0:T(8,128)(2,1)} %get-tuple-element.56) | copy-start | bytes 7864324
  73.6 18.8 %collective-permute-start.1 = (bf16[4,2,64,2048]{3,2,0,1:T(8,128)(2,1)}, bf16[4,2,64,2048]{3,2,0,1:T(8,128)(2,1)}, u32[]{:S(2)}, u32[]{:S(2)}) collective-permute-start(bf16[4,2,64,2048]{3,2,0,1:T(8,128)(2,1)} %fusion.9), channel_id=1, source_target_pairs={{0,1},{1,0},{2,3},{3,2},{4,5},{5,4},{6,7},{7,6},{8,9},{9,8},{10,11... | collective-permute-start | bytes 6291464 | tf_op jit(solution)/shard_map/ppermute | solution.py:291
  73.6 9.9 %copy-start.26 = (bf16[640,2048]{1,0:T(8,128)(2,1)S(1)}, bf16[640,2048]{1,0:T(8,128)(2,1)}, u32[]{:S(2)}) copy-start(bf16[640,2048]{1,0:T(8,128)(2,1)} %copy-done.25) | copy-start | bytes 7864324
  77.1 4.3 %copy-start.13 = (f32[2048,1024]{1,0:T(8,128)}, f32[2048,1024]{1,0:T(8,128)S(1)}, u32[]{:S(2)}) copy-start(f32[2048,1024]{1,0:T(8,128)S(1)} %convolution_multiply_fusion.1) | copy-start | bytes 25165828
  77.1 6.4 %copy-start.20 = (bf16[1024,2048]{1,0:T(8,128)(2,1)S(1)}, bf16[1024,2048]{1,0:T(8,128)(2,1)}, u32[]{:S(2)}) copy-start(bf16[1024,2048]{1,0:T(8,128)(2,1)} %param.19) | copy-start | bytes 12582916
  83.0 14.3 %collective-permute-start = (bf16[4,2,128,1024]{3,2,0,1:T(8,128)(2,1)}, bf16[4,2,128,1024]{3,2,0,1:T(8,128)(2,1)}, u32[]{:S(2)}, u32[]{:S(2)}) collective-permute-start(bf16[4,2,128,1024]{3,2,0,1:T(8,128)(2,1)} %fusion.8), channel_id=1, source_target_pairs={{0,1},{1,0},{2,3},{3,2},{4,5},{5,4},{6,7},{7,6},{8,9},{9,8},{10,11... | collective-permute-start | bytes 6291464 | tf_op jit(solution)/shard_map/ppermute | solution.py:291
  87.9 2.7 %copy-start.10 = (f32[640,1024]{1,0:T(8,128)S(1)}, f32[640,1024]{1,0:T(8,128)}, u32[]{:S(2)}) copy-start(f32[640,1024]{1,0:T(8,128)} %get-tuple-element.55) | copy-start | bytes 7864324
  90.6 6.8 %slice-start = ((s8[8388608]{0:T(1024)(128)(4,1)}), s8[4194304]{0:T(1024)(128)(4,1)S(1)}, s32[]{:S(2)}) async-start(s8[8388608]{0:T(1024)(128)(4,1)} %bitcast.89), calls=%async_computation | async-start | bytes 8388608
  92.4 5.0 %slice-start.1 = ((s8[8388608]{0:T(1024)(128)(4,1)}), s8[4194304]{0:T(1024)(128)(4,1)S(1)}, s32[]{:S(2)}) async-start(s8[8388608]{0:T(1024)(128)(4,1)} %bitcast.89), calls=%async_computation.1 | async-start | bytes 8388608
  96.0 4.5 %copy-start.7 = (f32[4,2,64,2048]{3,2,0,1:T(8,128)}, f32[4,2,64,2048]{3,2,0,1:T(8,128)S(1)}, u32[]{:S(2)}) copy-start(f32[4,2,64,2048]{3,2,0,1:T(8,128)S(1)} %bitcast_add_fusion) | copy-start | bytes 12582916
  97.3 12.5 %copy-start.1 = (f32[5,128,1024]{2,1,0:T(8,128)S(1)}, f32[5,128,1024]{2,1,0:T(8,128)}, u32[]{:S(2)}) copy-start(f32[5,128,1024]{2,1,0:T(8,128)} %copy-done) | copy-start | bytes 7864324
  97.3 12.5 %copy-start.22 = (bf16[2048,1024]{1,0:T(8,128)(2,1)S(1)}, bf16[2048,1024]{1,0:T(8,128)(2,1)}, u32[]{:S(2)}) copy-start(bf16[2048,1024]{1,0:T(8,128)(2,1)} %param.21) | copy-start | bytes 12582916
  97.3 12.5 %copy-start.24 = (f32[1024]{0:T(1024)S(1)}, f32[1024]{0:T(1024)}, u32[]{:S(2)}) copy-start(f32[1024]{0:T(1024)} %param.22) | copy-start | bytes 12292
  97.3 12.5 %copy-start.28 = (bf16[640,2048]{1,0:T(8,128)(2,1)S(1)}, bf16[640,2048]{1,0:T(8,128)(2,1)}, u32[]{:S(2)}) copy-start(bf16[640,2048]{1,0:T(8,128)(2,1)} %get-tuple-element.56) | copy-start | bytes 7864324
  100.4 2.5 copy-start.9
  102.9 91.5 %collective-permute-start.2 = (bf16[4,128,1024]{2,1,0:T(8,128)(2,1)}, bf16[4,128,1024]{2,1,0:T(8,128)(2,1)}, u32[]{:S(2)}, u32[]{:S(2)}) collective-permute-start(bf16[4,128,1024]{2,1,0:T(8,128)(2,1)} %fusion.10), channel_id=1, source_target_pairs={{0,2},{2,0},{4,6},{6,4},{8,10},{10,8},{12,14},{14,12},{1,3},{3,1},... | collective-permute-start | bytes 3145736 | tf_op jit(solution)/shard_map/ppermute | solution.py:291
  109.7 87.2 %collective-permute-start.3 = (bf16[4,64,2048]{2,1,0:T(8,128)(2,1)}, bf16[4,64,2048]{2,1,0:T(8,128)(2,1)}, u32[]{:S(2)}, u32[]{:S(2)}) collective-permute-start(bf16[4,64,2048]{2,1,0:T(8,128)(2,1)} %fusion.11), channel_id=1, source_target_pairs={{0,2},{2,0},{4,6},{6,4},{8,10},{10,8},{12,14},{14,12},{1,3},{3,1},... | collective-permute-start | bytes 3145736 | tf_op jit(solution)/shard_map/ppermute | solution.py:291
  113.1 1.3 copy-start.2
  193.3 1.1 copy-start.4
  194.4 3.1 %copy-start.8 = (f32[4,2,64,2048]{3,2,0,1:T(8,128)S(1)}, f32[4,2,64,2048]{3,2,0,1:T(8,128)}, u32[]{:S(2)}) copy-start(f32[4,2,64,2048]{3,2,0,1:T(8,128)} %copy-done.7) | copy-start | bytes 12582916
  196.9 2.3 copy-start.11
  199.2 1.3 copy-start.12
  200.5 12.0 %collective-permute-start.4 = (f32[56,1024]{1,0:T(8,128)S(1)}, f32[56,1024]{1,0:T(8,128)S(1)}, u32[]{:S(2)}, u32[]{:S(2)}) collective-permute-start(f32[56,1024]{1,0:T(8,128)S(1)} %concatenate.3), channel_id=1, source_target_pairs={{0,1},{1,0},{2,3},{3,2},{4,5},{5,4},{6,7},{7,6},{8,9},{9,8},{10,11... | collective-permute-start | bytes 688136 | tf_op jit(solution)/shard_map/ppermute | solution.py:328
  200.5 18.8 %collective-permute-start.8 = (bf16[64,2048]{1,0:T(8,128)(2,1)S(1)}, bf16[64,2048]{1,0:T(8,128)(2,1)S(1)}, u32[]{:S(2)}, u32[]{:S(2)}) collective-permute-start(bf16[64,2048]{1,0:T(8,128)(2,1)S(1)} %get-tuple-element.32), channel_id=1, source_target_pairs={{0,4},{2,6},{4,8},{6,10},{8,12},{10,14},{12,0},{14,2},{1,5},{3,7},... | collective-permute-start | bytes 786440 | tf_op jit(solution)/shard_map/ppermute | solution.py:291
  208.6 19.5 %collective-permute-start.9 = (bf16[64,2048]{1,0:T(8,128)(2,1)S(1)}, bf16[64,2048]{1,0:T(8,128)(2,1)}, u32[]{:S(2)}, u32[]{:S(2)}) collective-permute-start(bf16[64,2048]{1,0:T(8,128)(2,1)S(1)} %get-tuple-element.33), channel_id=1, source_target_pairs={{0,8},{2,10},{4,12},{6,14},{8,0},{10,2},{12,4},{14,6},{1,9},{3,11}... | collective-permute-start | bytes 786440 | tf_op jit(solution)/shard_map/ppermute | solution.py:291
  210.0 34.4 %collective-permute-start.10 = (bf16[64,2048]{1,0:T(8,128)(2,1)S(1)}, bf16[64,2048]{1,0:T(8,128)(2,1)}, u32[]{:S(2)}, u32[]{:S(2)}) collective-permute-start(bf16[64,2048]{1,0:T(8,128)(2,1)S(1)} %get-tuple-element.34), channel_id=1, source_target_pairs={{0,12},{2,14},{4,0},{6,2},{8,4},{10,6},{12,8},{14,10},{1,13},{3,15... | collective-permute-start | bytes 786440 | tf_op jit(solution)/shard_map/ppermute | solution.py:291
  212.5 6.7 %collective-permute-start.5 = (f32[56,1024]{1,0:T(8,128)S(1)}, f32[56,1024]{1,0:T(8,128)S(1)}, u32[]{:S(2)}, u32[]{:S(2)}) collective-permute-start(f32[56,1024]{1,0:T(8,128)S(1)} %add.239), channel_id=1, source_target_pairs={{0,2},{2,0},{4,6},{6,4},{8,10},{10,8},{12,14},{14,12},{1,3},{3,1},... | collective-permute-start | bytes 688136 | tf_op jit(solution)/shard_map/ppermute | solution.py:328
  213.0 41.1 %collective-permute-start.11 = (bf16[128,1024]{1,0:T(8,128)(2,1)S(1)}, bf16[128,1024]{1,0:T(8,128)(2,1)S(1)}, u32[]{:S(2)}, u32[]{:S(2)}) collective-permute-start(bf16[128,1024]{1,0:T(8,128)(2,1)S(1)} %get-tuple-element.35), channel_id=1, source_target_pairs={{0,4},{2,6},{4,8},{6,10},{8,12},{10,14},{12,0},{14,2},{1,5},{3,7},... | collective-permute-start | bytes 786440 | tf_op jit(solution)/shard_map/ppermute | solution.py:291
  219.3 34.8 %collective-permute-start.12 = (bf16[128,1024]{1,0:T(8,128)(2,1)S(1)}, bf16[128,1024]{1,0:T(8,128)(2,1)S(1)}, u32[]{:S(2)}, u32[]{:S(2)}) collective-permute-start(bf16[128,1024]{1,0:T(8,128)(2,1)S(1)} %get-tuple-element.36), channel_id=1, source_target_pairs={{0,8},{2,10},{4,12},{6,14},{8,0},{10,2},{12,4},{14,6},{1,9},{3,11}... | collective-permute-start | bytes 786440 | tf_op jit(solution)/shard_map/ppermute | solution.py:291
  219.3 47.9 %copy-start.5 = (bf16[5,128,1024]{2,1,0:T(8,128)(2,1)S(1)}, bf16[5,128,1024]{2,1,0:T(8,128)(2,1)}, u32[]{:S(2)}) copy-start(bf16[5,128,1024]{2,1,0:T(8,128)(2,1)} %copy-done.4) | copy-start | bytes 3932164
  219.3 34.8 %collective-permute-start.13 = (bf16[128,1024]{1,0:T(8,128)(2,1)S(1)}, bf16[128,1024]{1,0:T(8,128)(2,1)S(1)}, u32[]{:S(2)}, u32[]{:S(2)}) collective-permute-start(bf16[128,1024]{1,0:T(8,128)(2,1)S(1)} %get-tuple-element.37), channel_id=1, source_target_pairs={{0,12},{2,14},{4,0},{6,2},{8,4},{10,6},{12,8},{14,10},{1,13},{3,15... | collective-permute-start | bytes 786440 | tf_op jit(solution)/shard_map/ppermute | solution.py:291
  228.1 24.1 %collective-permute-start.6 = (f32[56,1024]{1,0:T(8,128)S(1)}, f32[56,1024]{1,0:T(8,128)S(1)}, u32[]{:S(2)}, u32[]{:S(2)}) collective-permute-start(f32[56,1024]{1,0:T(8,128)S(1)} %add.240), channel_id=1, source_target_pairs={{0,4},{2,6},{4,0},{6,2},{8,12},{10,14},{12,8},{14,10},{1,5},{3,7},... | collective-permute-start | bytes 688136 | tf_op jit(solution)/shard_map/ppermute | solution.py:328
  252.2 13.0 %collective-permute-start.7 = (f32[56,1024]{1,0:T(8,128)S(1)}, f32[56,1024]{1,0:T(8,128)S(1)}, u32[]{:S(2)}, u32[]{:S(2)}) collective-permute-start(f32[56,1024]{1,0:T(8,128)S(1)} %add.241), channel_id=1, source_target_pairs={{0,8},{2,10},{4,12},{6,14},{8,0},{10,2},{12,4},{14,6},{1,9},{3,11}... | collective-permute-start | bytes 688136 | tf_op jit(solution)/shard_map/ppermute | solution.py:328

commit v2 on v1

--- a/solution.py
+++ b/solution.py
@@ -292,26 +292,27 @@
     return own
 
 
-def over_cores(partial):
+def over_cores(partial, high_first):
     rows, cols = (lax.axis_size("rows"), lax.axis_size("cols"))
     high, low = split_rows(rows)
     block = partial.shape[0] // (rows * cols)
     value = partial.reshape(high, low, cols, block, partial.shape[1])
     own, theirs = pick(value, 2, cols, lax.axis_index("cols"))
     value = exchange(own, theirs, "cols", lambda k: [(i, (i + k) % cols) for i in range(cols)])
+    if high_first:
+        return pick(value, 0, high, lax.axis_index("rows") // low)
     return pick(value, 1, low, lax.axis_index("rows") % low)
 
 
 def over_low(own, theirs):
     rows = lax.axis_size("rows")
-    high, low = split_rows(rows)
-    value = exchange(
+    _, low = split_rows(rows)
+    return exchange(
         own,
         theirs,
         "rows",
         lambda k: [(i, i // low * low + (i % low + k) % low) for i in range(rows)],
     )
-    return pick(value, 0, high, lax.axis_index("rows") // low)
 
 
 def over_high(own, theirs):
@@ -404,13 +405,15 @@
         lax.dot_general(
             act, branch_grad, (((0,), (0,)), ((), ())), preferred_element_type=jnp.float32
         )
-        * factor
-    )
-    expand_low, expand_sent = over_cores(
+        * factor,
+        False,
+    )
+    expand_high, expand_sent = over_cores(
         lax.dot_general(
             normed, pre_grad, (((0,), (0,)), ((), ())), preferred_element_type=jnp.float32
         )
-        * factor
+        * factor,
+        True,
     )
     mixed_grad, project_sent, expand_sent = lax.optimization_barrier(
         (mixed_grad, project_sent, expand_sent)
@@ -440,14 +443,16 @@
         jnp.sum(masked * out_branch, axis=0),
     )
     packed = jnp.concatenate([value.reshape(-1, width) for value in local_sums], axis=0)
-    project_high, project_sent = over_low(project_low, project_sent)
-    expand_high, expand_sent = over_low(expand_low, expand_sent)
+    high, low = split_rows(row_count)
+    row = lax.axis_index("rows")
+    project_high, project_sent = pick(over_low(project_low, project_sent), 0, high, row // low)
+    expand_low, expand_sent = pick(over_high(expand_high, expand_sent), 0, low, row % low)
     packed, project_sent, expand_sent = lax.optimization_barrier(
         (packed, project_sent, expand_sent)
     )
     packed = whole_sum(packed) * factor
     project_grad = over_high(project_high, project_sent)
-    expand_grad = over_high(expand_high, expand_sent)
+    expand_grad = over_low(expand_low, expand_sent)
     hidden = expand.shape[1]
     depthwise_grad = packed[:49].reshape(7, 7, width)
     depthbias_grad = packed[49]

time: 269 us -> 230 us (0.86)
  Pallas kernels: 122 us -> 99 us
  starting transfers between devices: 40 us -> 28.8 us
    pallas_call x1, Pallas kernels: 78.9 us -> 55.7 us  [per_device(): halo_call(backward_kernel, features.shape, [jax.ShapeDtypeStruct(features...]
    ppermute x4, starting transfers between devices: 18.6 us -> 4.34 us  [whole_sum(): lax.ppermute(value, axis, [(i, i ^ bit) for i in range(size)])]
    ppermute x4, waiting for transfers between devices: 21.1 us -> 29 us  [whole_sum(): lax.ppermute(value, axis, [(i, i ^ bit) for i in range(size)])]
    ppermute x10, waiting for transfers between devices: 6.77 us -> 0.03 us  [exchange(): own = own + lax.ppermute(part, axis, perm_of(step)).astype(jnp.float32)]
    ppermute x10, starting transfers between devices: 21.4 us -> 24.4 us  [exchange(): own = own + lax.ppermute(part, axis, perm_of(step)).astype(jnp.float32)]
    unnamed x65 -> x55, local copies, waits for them, and re-layouts: 14.8 us -> 15.8 us
  transfers between devices with their start and end apart: 14 -> 14, of which waited for: 4 -> 3; matrix products, arithmetic and copies ran while one was open for 11% -> 14% of each run, Pallas kernels for 29% -> 24%
where the time goes in v2:
time: 230 us
  Pallas kernels  99 us (43%)
  waiting for transfers between devices  29 us (13%)
  starting transfers between devices  28.8 us (13%)
  matrix products  25.9 us (11%)
  local copies, waits for them, and re-layouts  24.4 us (11%)
  other arithmetic  21.2 us (9%)
    pallas_call x1, Pallas kernels, per_device(): halo_call(backward_kernel, features.shape, [jax.ShapeDtypeStruct(features...  55.7 us
    pallas_call x1, Pallas kernels, per_device(): halo_call(forward_kernel, features.shape, [jax.ShapeDtypeStruct(features....  43.3 us
    ppermute x4, waiting for transfers between devices, whole_sum(): lax.ppermute(value, axis, [(i, i ^ bit) for i in range(size)])  29 us
    ppermute x10, starting transfers between devices, exchange(): own = own + lax.ppermute(part, axis, perm_of(step)).astype(jnp.float32)  24.4 us
    unnamed x55, local copies, waits for them, and re-layouts  15.8 us
    add x6, other arithmetic, exchange(): own = own + lax.ppermute(part, axis, perm_of(step)).astype(jnp.float32)  12.1 us
    convert_element_type x6, local copies, waits for them, and re-layouts, pick(): lax.dynamic_index_in_dim(value, (place + step) % size, dim, keepdims=False)  5.98 us
    dot_general x1, matrix products, per_device(): lax.dot_general(branch_grad, project, (((1,), (1,)), ((), ())), preferred...  5.31 us
  transfers between devices with their start and end apart: 14, of which 3 were waited for; matrix products, arithmetic and copies ran while one was open for 14% of the time, Pallas kernels for 24%

profile of v2, /device:TPU:0, one launch (start us, length us, event | category | flops | bytes accessed | tf_op | source)
XLA Modules:
  0.0 229.5 jit_solution(12053381269696086843)
XLA Ops:
  0.7 0.9 reshape.200.weight
  1.6 0.9 fusion.24
  2.5 0.2 fusion.22
  2.7 1.8 convert_reduce_fusion.1
  4.6 0.0 copy-start.3
  4.6 1.4 fusion.6
  6.0 0.5 copy-done
  6.5 0.3 copy-done.3
  6.9 43.3 %shard_map.195 = (f32[5,128,1024]{2,1,0:T(8,128)S(1)}, bf16[11,160,1024]{2,1,0:T(8,128)(2,1)}) custom-call(bf16[5,128,1024]{2,1,0:T(8,128)(2,1)S(1)} %copy-done.3, f32[49,1024]{1,0:T(8,128)S(1)} %reshape.200.weight, f32[1,1024]{1,0:T(1,128)S(1)} %bitcast.87), custom_call_target="tpu_custom_call" | custom-call | flops 64225280 | bytes 8388608 | tf_op jit(solution)/shard_map/pallas_call | solution.py:353
  50.2 0.2 reduce_sum.90
  50.4 0.4 multiply_reduce_fusion.3
  50.8 0.0 copy-done.14
  50.8 0.0 copy-done.16
  50.9 0.5 add_convert_fusion
  51.3 0.1 copy-done.20
  51.5 5.2 %multiply_convert_fusion = (bf16[640,2048]{1,0:T(8,128)(2,1)S(1)}, f32[640,2048]{1,0:T(8,128)S(1)}) fusion(f32[2048]{0:T(1024)S(1)} %copy-done.20, bf16[640,1024]{1,0:T(8,128)(2,1)S(1)} %bitcast.96, bf16[1024,2048]{1,0:T(8,128)(2,1)} %param.19), kind=kOutput, calls=%fused_computation.8 | convolution fusion | flops 2692218880 | bytes 13377536 | tf_op jit(solution)/shard_map/dot_general | solution.py:368
  56.7 3.5 %convolution_multiply_fusion.1 = f32[2048,1024]{1,0:T(8,128)S(1)} fusion(bf16[640,2048]{1,0:T(8,128)(2,1)S(1)} %get-tuple-element.56, bf16[640,1024]{1,0:T(8,128)(2,1)S(1)} %copy-done.13), kind=kOutput, calls=%fused_computation.11 | convolution fusion | flops 2686451712 | bytes 12320768 | tf_op jit(solution)/shard_map/dot_general | solution.py:405
  60.3 4.2 %copy-done.11 = f32[2048,1024]{1,0:T(8,128)} copy-done((f32[2048,1024]{1,0:T(8,128)}, f32[2048,1024]{1,0:T(8,128)S(1)}, u32[]{:S(2)}) %copy-start.11) | copy-done | bytes 8388632
  64.5 1.6 fusion.8
  66.1 5.3 %convert_reduce_fusion = (f32[2048]{0:T(1024)S(1)}, bf16[640,2048]{1,0:T(8,128)(2,1)S(1)}) fusion(f32[640,2048]{1,0:T(8,128)S(1)} %get-tuple-element.57, f32[2048]{0:T(1024)S(1)} %copy-done.20, bf16[640,1024]{1,0:T(8,128)(2,1)S(1)} %copy-done.13, bf16[2048,1024]{1,0:T(8,128)(2,1)S(1)} %copy-done.18), kind=kOutput, calls=%fused_computation.7 | convolution fusion | flops 2701391872 | bytes 13385728 | tf_op jit(solution)/shard_map/dot_general | solution.py:386
  71.5 3.5 %convolution_multiply_fusion = f32[1024,2048]{1,0:T(8,128)S(1)} fusion(bf16[640,1024]{1,0:T(8,128)(2,1)S(1)} %bitcast.97, bf16[640,2048]{1,0:T(8,128)(2,1)S(1)} %get-tuple-element.59), kind=kOutput, calls=%fused_computation.10 | convolution fusion | flops 2686451712 | bytes 12320768 | tf_op jit(solution)/shard_map/dot_general | solution.py:412
  75.0 4.2 %copy-done.12 = f32[1024,2048]{1,0:T(8,128)} copy-done((f32[1024,2048]{1,0:T(8,128)}, f32[1024,2048]{1,0:T(8,128)S(1)}, u32[]{:S(2)}) %copy-start.12) | copy-done | bytes 8388632
  79.2 1.6 fusion.9
  80.8 0.5 collective-permute-start.1
  81.3 4.4 %fusion.27 = (f32[1024]{0:T(1024)S(1)}, f32[640]{0:T(1024)S(1)}, f32[640,1024]{1,0:T(8,128)}) fusion(f32[1024]{0:T(1024)S(1)} %copy-done.14, bf16[640,2048]{1,0:T(8,128)(2,1)S(1)} %get-tuple-element.59, bf16[1024,2048]{1,0:T(8,128)(2,1)S(1)} %copy-done.17), kind=kOutput, calls=%fused_computation.81 | convolution fusion | flops 2686319104 | bytes 9447936 | tf_op jit(solution)/shard_map/dot_general | solution.py:391
  85.7 2.7 %multiply_reduce_fusion = (f32[1024]{0:T(1024)S(1)}, f32[5,128]{1,0:T(8,128)S(1)}) fusion(f32[5,128,1024]{2,1,0:T(8,128)} %bitcast.88, f32[5,128,1024]{2,1,0:T(8,128)S(1)} %get-tuple-element.24, f32[5,128]{1,0:T(8,128)S(1)} %add_rsqrt_fusion, f32[5,128]{1,0:T(8,128)S(1)} %broadcast_multiply_fusion.1, f32[1024]{0:T(1024)S(1)} %copy-done.14), kind=kLoop, calls=%fused_computation.22 | loop fusion | flops 4585856 | bytes 5258752 | tf_op jit(solution)/shard_map/reduce_sum | solution.py:439
  88.5 1.8 multiply_convert_fusion.2.own
  90.3 3.7 %bitcast_add_fusion.1 = f32[4,2,128,1024]{3,2,0,1:T(8,128)S(1)} fusion(bf16[4,2,128,1024]{3,2,0,1:T(8,128)(2,1)} %collective-permute-done, f32[4,2,2,128,1024]{4,3,2,1,0:T(8,128)} %bitcast.91, s32[]{:T(128)S(6)} %select_n.104), kind=kLoop, calls=%fused_computation.15 | loop fusion | flops 2097152 | bytes 10485764 | tf_op jit(solution)/shard_map/add | solution.py:291
  93.9 1.4 fusion.10
  95.4 2.8 %bitcast_add_fusion = f32[4,2,64,2048]{3,2,1,0:T(8,128)S(1)} fusion(bf16[4,2,64,2048]{3,2,1,0:T(8,128)(2,1)} %collective-permute-done.1, f32[4,2,2,64,2048]{4,3,2,1,0:T(8,128)S(1)} %bitcast.95, s32[]{:T(128)S(6)} %select_n.104), kind=kLoop, calls=%fused_computation.14 | loop fusion | flops 2097152 | bytes 10485764 | tf_op jit(solution)/shard_map/add | solution.py:291
  98.3 1.2 fusion.15
  99.4 1.7 copy-done.9
  101.1 8.2 %collective-permute-start.3 = (bf16[2,64,2048]{2,1,0:T(8,128)(2,1)}, bf16[2,64,2048]{2,1,0:T(8,128)(2,1)}, u32[]{:S(2)}, u32[]{:S(2)}) collective-permute-start(bf16[2,64,2048]{2,1,0:T(8,128)(2,1)} %get-tuple-element.30), channel_id=1, source_target_pairs={{0,4},{2,6},{4,8},{6,10},{8,12},{10,14},{12,0},{14,2},{1,5},{3,7},... | collective-permute-start | bytes 1572872 | tf_op jit(solution)/shard_map/ppermute | solution.py:291
  109.3 1.3 collective-permute-start.4
  110.6 2.7 %collective-permute-start.5 = (bf16[2,64,2048]{2,1,0:T(8,128)(2,1)}, bf16[2,64,2048]{2,1,0:T(8,128)(2,1)}, u32[]{:S(2)}, u32[]{:S(2)}) collective-permute-start(bf16[2,64,2048]{2,1,0:T(8,128)(2,1)} %get-tuple-element.32), channel_id=1, source_target_pairs={{0,12},{2,14},{4,0},{6,2},{8,4},{10,6},{12,8},{14,10},{1,13},{3,15... | collective-permute-start | bytes 1572872 | tf_op jit(solution)/shard_map/ppermute | solution.py:291
  113.2 0.2 collective-permute-start.2
  113.5 2.9 %fusion.7 = f32[1024]{0:T(1024)S(1)} fusion(f32[5,128,1024]{2,1,0:T(8,128)S(1)} %copy-done.1, bf16[640,2048]{1,0:T(8,128)(2,1)S(1)} %copy-done.23, bf16[2048,1024]{1,0:T(8,128)(2,1)S(1)} %copy-done.19, f32[1024]{0:T(1024)S(1)} %copy-done.21), kind=kOutput, calls=%fused_computation.19 | convolution fusion | flops 2686319616 | bytes 9445376 | tf_op jit(solution)/shard_map/dot_general | solution.py:371
  116.4 0.3 rev.3.weight
  116.7 1.3 copy-done.2
  118.0 55.7 %shard_map.196 = (bf16[5,128,1024]{2,1,0:T(8,128)(2,1)S(1)}, f32[49,1024]{1,0:T(8,128)S(1)}) custom-call(bf16[5,128,1024]{2,1,0:T(8,128)(2,1)S(1)} %copy-done.2, f32[49,1024]{1,0:T(8,128)S(1)} %rev.3.weight, f32[5,128,1024]{2,1,0:T(8,128)S(1)} %copy-done.1, bf16[11,160,1024]{2,1,0:T(8,128)(2,1)} %get-tuple-element.26.features), custom_call_target="tpu_custom_call" | custom-call | flops 128450560 | bytes 8388608 | tf_op jit(solution)/shard_map/pallas_call | solution.py:421
  173.7 0.2 convert_reduce_fusion.2
  173.9 0.8 copy-done.4
  174.8 0.1 concatenate.3
  174.9 2.1 fusion.12
  177.1 0.8 copy-done.8
  177.8 1.7 bitcast_add_fusion.2
  179.5 0.1 fusion.20
  179.6 0.1 collective-permute-start.6
  179.7 6.9 %collective-permute-start.10 = (bf16[64,2048]{1,0:T(8,128)(2,1)S(1)}, bf16[64,2048]{1,0:T(8,128)(2,1)S(1)}, u32[]{:S(2)}, u32[]{:S(2)}) collective-permute-start(bf16[64,2048]{1,0:T(8,128)(2,1)S(1)} %fusion.21), channel_id=1, source_target_pairs={{0,2},{2,0},{4,6},{6,4},{8,10},{10,8},{12,14},{14,12},{1,3},{3,1},... | collective-permute-start | bytes 786440 | tf_op jit(solution)/shard_map/ppermute | solution.py:291
  186.6 1.2 collective-permute-start.7
  187.8 1.7 collective-permute-start.11
  189.5 0.1 collective-permute-start.12
  189.6 2.9 %collective-permute-start.13 = (bf16[128,1024]{1,0:T(8,128)(2,1)S(1)}, bf16[128,1024]{1,0:T(8,128)(2,1)S(1)}, u32[]{:S(2)}, u32[]{:S(2)}) collective-permute-start(bf16[128,1024]{1,0:T(8,128)(2,1)S(1)} %get-tuple-element.37), channel_id=1, source_target_pairs={{0,12},{2,14},{4,0},{6,2},{8,4},{10,6},{12,8},{14,10},{1,13},{3,15... | collective-permute-start | bytes 786440 | tf_op jit(solution)/shard_map/ppermute | solution.py:291
  192.5 5.5 %collective-permute-done.7 = f32[56,1024]{1,0:T(8,128)S(1)} collective-permute-done((f32[56,1024]{1,0:T(8,128)S(1)}, f32[56,1024]{1,0:T(8,128)S(1)}, u32[]{:S(2)}, u32[]{:S(2)}) %collective-permute-start.7) | collective-permute-done | bytes 229408 | tf_op jit(solution)/shard_map/ppermute | solution.py:329
  198.1 1.9 collective-permute-start.8
  199.9 0.8 bitcast_add_fusion.5
  200.8 13.2 %collective-permute-done.8 = f32[56,1024]{1,0:T(8,128)S(1)} collective-permute-done((f32[56,1024]{1,0:T(8,128)S(1)}, f32[56,1024]{1,0:T(8,128)S(1)}, u32[]{:S(2)}, u32[]{:S(2)}) %collective-permute-start.8) | collective-permute-done | bytes 229408 | tf_op jit(solution)/shard_map/ppermute | solution.py:329
  214.1 1.2 collective-permute-start.9
  215.3 0.9 fusion.17
  216.2 10.3 %collective-permute-done.9 = f32[56,1024]{1,0:T(8,128)S(1)} collective-permute-done((f32[56,1024]{1,0:T(8,128)S(1)}, f32[56,1024]{1,0:T(8,128)S(1)}, u32[]{:S(2)}, u32[]{:S(2)}) %collective-permute-start.9) | collective-permute-done | bytes 229408 | tf_op jit(solution)/shard_map/ppermute | solution.py:329
  226.5 0.6 fusion.28
  227.2 0.6 copy.33
  227.8 0.7 reshape.197
  228.5 1.1 copy.35
  (66 shorter events, 0.4 us)
Async XLA Ops:
  0.6 3.9 %copy-start.15 = (f32[1024]{0:T(1024)S(1)}, f32[1024]{0:T(1024)}, u32[]{:S(2)}) copy-start(f32[1024]{0:T(1024)} %param.23) | copy-start | bytes 12292
  4.5 2.0 copy-start
  4.6 2.3 copy-start.3
  4.6 2.3 copy-start.6
  50.1 0.7 copy-start.14
  50.2 0.7 copy-start.16
  50.8 0.7 copy-start.20
  51.5 5.2 %copy-start.13 = (bf16[640,1024]{1,0:T(8,128)(2,1)S(1)}, bf16[640,1024]{1,0:T(8,128)(2,1)}, u32[]{:S(2)}) copy-start(bf16[640,1024]{1,0:T(8,128)(2,1)} %fusion.6) | copy-start | bytes 3932164
  56.7 3.6 %copy-start.22 = (bf16[640,2048]{1,0:T(8,128)(2,1)}, bf16[640,2048]{1,0:T(8,128)(2,1)S(1)}, u32[]{:S(2)}) copy-start(bf16[640,2048]{1,0:T(8,128)(2,1)S(1)} %get-tuple-element.56) | copy-start | bytes 7864324
  60.3 4.3 %copy-start.11 = (f32[2048,1024]{1,0:T(8,128)}, f32[2048,1024]{1,0:T(8,128)S(1)}, u32[]{:S(2)}) copy-start(f32[2048,1024]{1,0:T(8,128)S(1)} %convolution_multiply_fusion.1) | copy-start | bytes 25165828
  60.3 5.9 %copy-start.18 = (bf16[2048,1024]{1,0:T(8,128)(2,1)S(1)}, bf16[2048,1024]{1,0:T(8,128)(2,1)}, u32[]{:S(2)}) copy-start(bf16[2048,1024]{1,0:T(8,128)(2,1)} %param.21) | copy-start | bytes 12582916
  66.1 24.1 %collective-permute-start = (bf16[4,2,128,1024]{3,2,0,1:T(8,128)(2,1)}, bf16[4,2,128,1024]{3,2,0,1:T(8,128)(2,1)}, u32[]{:S(2)}, u32[]{:S(2)}) collective-permute-start(bf16[4,2,128,1024]{3,2,0,1:T(8,128)(2,1)} %fusion.8), channel_id=1, source_target_pairs={{0,1},{1,0},{2,3},{3,2},{4,5},{5,4},{6,7},{7,6},{8,9},{9,8},{10,11... | collective-permute-start | bytes 6291464 | tf_op jit(solution)/shard_map/ppermute | solution.py:291
  75.0 4.3 %copy-start.12 = (f32[1024,2048]{1,0:T(8,128)}, f32[1024,2048]{1,0:T(8,128)S(1)}, u32[]{:S(2)}) copy-start(f32[1024,2048]{1,0:T(8,128)S(1)} %convolution_multiply_fusion) | copy-start | bytes 25165828
  75.0 6.4 %copy-start.17 = (bf16[1024,2048]{1,0:T(8,128)(2,1)S(1)}, bf16[1024,2048]{1,0:T(8,128)(2,1)}, u32[]{:S(2)}) copy-start(bf16[1024,2048]{1,0:T(8,128)(2,1)} %param.19) | copy-start | bytes 12582916
  80.8 14.5 %collective-permute-start.1 = (bf16[4,2,64,2048]{3,2,1,0:T(8,128)(2,1)}, bf16[4,2,64,2048]{3,2,1,0:T(8,128)(2,1)}, u32[]{:S(2)}, u32[]{:S(2)}) collective-permute-start(bf16[4,2,64,2048]{3,2,1,0:T(8,128)(2,1)} %fusion.9), channel_id=1, source_target_pairs={{0,1},{1,0},{2,3},{3,2},{4,5},{5,4},{6,7},{7,6},{8,9},{9,8},{10,11... | collective-permute-start | bytes 6291464 | tf_op jit(solution)/shard_map/ppermute | solution.py:291
  85.7 2.7 %copy-start.10 = (f32[640,1024]{1,0:T(8,128)S(1)}, f32[640,1024]{1,0:T(8,128)}, u32[]{:S(2)}) copy-start(f32[640,1024]{1,0:T(8,128)} %get-tuple-element.55) | copy-start | bytes 7864324
  88.4 6.9 %slice-start = ((s8[8388608]{0:T(1024)(128)(4,1)}), s8[4194304]{0:T(1024)(128)(4,1)S(1)}, s32[]{:S(2)}) async-start(s8[8388608]{0:T(1024)(128)(4,1)} %bitcast.93), calls=%async_computation | async-start | bytes 8388608
  90.2 5.1 %slice-start.1 = ((s8[8388608]{0:T(1024)(128)(4,1)}), s8[4194304]{0:T(1024)(128)(4,1)S(1)}, s32[]{:S(2)}) async-start(s8[8388608]{0:T(1024)(128)(4,1)} %bitcast.93), calls=%async_computation.1 | async-start | bytes 8388608
  93.9 4.3 %copy-start.7 = (f32[4,2,128,1024]{3,2,0,1:T(8,128)}, f32[4,2,128,1024]{3,2,0,1:T(8,128)S(1)}, u32[]{:S(2)}) copy-start(f32[4,2,128,1024]{3,2,0,1:T(8,128)S(1)} %bitcast_add_fusion.1) | copy-start | bytes 12582916
  95.4 18.1 %copy-start.19 = (bf16[2048,1024]{1,0:T(8,128)(2,1)S(1)}, bf16[2048,1024]{1,0:T(8,128)(2,1)}, u32[]{:S(2)}) copy-start(bf16[2048,1024]{1,0:T(8,128)(2,1)} %param.21) | copy-start | bytes 12582916
  95.4 18.1 %copy-start.23 = (bf16[640,2048]{1,0:T(8,128)(2,1)S(1)}, bf16[640,2048]{1,0:T(8,128)(2,1)}, u32[]{:S(2)}) copy-start(bf16[640,2048]{1,0:T(8,128)(2,1)} %copy-done.22) | copy-start | bytes 7864324
  98.2 2.9 %copy-start.9 = (f32[4,2,64,2048]{3,2,1,0:T(8,128)}, f32[4,2,64,2048]{3,2,1,0:T(8,128)S(1)}, u32[]{:S(2)}) copy-start(f32[4,2,64,2048]{3,2,1,0:T(8,128)S(1)} %bitcast_add_fusion) | copy-start | bytes 12582916
  98.2 15.2 %copy-start.1 = (f32[5,128,1024]{2,1,0:T(8,128)S(1)}, f32[5,128,1024]{2,1,0:T(8,128)}, u32[]{:S(2)}) copy-start(f32[5,128,1024]{2,1,0:T(8,128)} %copy-done) | copy-start | bytes 7864324
  98.2 15.2 %copy-start.21 = (f32[1024]{0:T(1024)S(1)}, f32[1024]{0:T(1024)}, u32[]{:S(2)}) copy-start(f32[1024]{0:T(1024)} %param.22) | copy-start | bytes 12292
  101.1 73.7 %collective-permute-start.3 = (bf16[2,64,2048]{2,1,0:T(8,128)(2,1)}, bf16[2,64,2048]{2,1,0:T(8,128)(2,1)}, u32[]{:S(2)}, u32[]{:S(2)}) collective-permute-start(bf16[2,64,2048]{2,1,0:T(8,128)(2,1)} %get-tuple-element.30), channel_id=1, source_target_pairs={{0,4},{2,6},{4,8},{6,10},{8,12},{10,14},{12,0},{14,2},{1,5},{3,7},... | collective-permute-start | bytes 1572872 | tf_op jit(solution)/shard_map/ppermute | solution.py:291
  109.3 65.5 %collective-permute-start.4 = (bf16[2,64,2048]{2,1,0:T(8,128)(2,1)}, bf16[2,64,2048]{2,1,0:T(8,128)(2,1)}, u32[]{:S(2)}, u32[]{:S(2)}) collective-permute-start(bf16[2,64,2048]{2,1,0:T(8,128)(2,1)} %get-tuple-element.31), channel_id=1, source_target_pairs={{0,8},{2,10},{4,12},{6,14},{8,0},{10,2},{12,4},{14,6},{1,9},{3,11}... | collective-permute-start | bytes 1572872 | tf_op jit(solution)/shard_map/ppermute | solution.py:291
  110.6 64.3 %collective-permute-start.5 = (bf16[2,64,2048]{2,1,0:T(8,128)(2,1)}, bf16[2,64,2048]{2,1,0:T(8,128)(2,1)}, u32[]{:S(2)}, u32[]{:S(2)}) collective-permute-start(bf16[2,64,2048]{2,1,0:T(8,128)(2,1)} %get-tuple-element.32), channel_id=1, source_target_pairs={{0,12},{2,14},{4,0},{6,2},{8,4},{10,6},{12,8},{14,10},{1,13},{3,15... | collective-permute-start | bytes 1572872 | tf_op jit(solution)/shard_map/ppermute | solution.py:291
  113.2 63.8 %collective-permute-start.2 = (bf16[4,128,1024]{2,1,0:T(8,128)(2,1)}, bf16[4,128,1024]{2,1,0:T(8,128)(2,1)}, u32[]{:S(2)}, u32[]{:S(2)}) collective-permute-start(bf16[4,128,1024]{2,1,0:T(8,128)(2,1)} %fusion.10), channel_id=1, source_target_pairs={{0,2},{2,0},{4,6},{6,4},{8,10},{10,8},{12,14},{14,12},{1,3},{3,1},... | collective-permute-start | bytes 3145736 | tf_op jit(solution)/shard_map/ppermute | solution.py:291
  116.7 1.3 copy-start.2
  173.7 1.1 copy-start.4
  174.8 3.0 %copy-start.8 = (f32[4,2,128,1024]{3,2,0,1:T(8,128)S(1)}, f32[4,2,128,1024]{3,2,0,1:T(8,128)}, u32[]{:S(2)}) copy-start(f32[4,2,128,1024]{3,2,0,1:T(8,128)} %copy-done.7) | copy-start | bytes 12582916
  179.6 6.9 %collective-permute-start.6 = (f32[56,1024]{1,0:T(8,128)S(1)}, f32[56,1024]{1,0:T(8,128)S(1)}, u32[]{:S(2)}, u32[]{:S(2)}) collective-permute-start(f32[56,1024]{1,0:T(8,128)S(1)} %concatenate.3), channel_id=1, source_target_pairs={{0,1},{1,0},{2,3},{3,2},{4,5},{5,4},{6,7},{7,6},{8,9},{9,8},{10,11... | collective-permute-start | bytes 688136 | tf_op jit(solution)/shard_map/ppermute | solution.py:329
  179.7 20.2 %collective-permute-start.10 = (bf16[64,2048]{1,0:T(8,128)(2,1)S(1)}, bf16[64,2048]{1,0:T(8,128)(2,1)S(1)}, u32[]{:S(2)}, u32[]{:S(2)}) collective-permute-start(bf16[64,2048]{1,0:T(8,128)(2,1)S(1)} %fusion.21), channel_id=1, source_target_pairs={{0,2},{2,0},{4,6},{6,4},{8,10},{10,8},{12,14},{14,12},{1,3},{3,1},... | collective-permute-start | bytes 786440 | tf_op jit(solution)/shard_map/ppermute | solution.py:291
  186.6 11.4 %collective-permute-start.7 = (f32[56,1024]{1,0:T(8,128)S(1)}, f32[56,1024]{1,0:T(8,128)S(1)}, u32[]{:S(2)}, u32[]{:S(2)}) collective-permute-start(f32[56,1024]{1,0:T(8,128)S(1)} %add.242), channel_id=1, source_target_pairs={{0,2},{2,0},{4,6},{6,4},{8,10},{10,8},{12,14},{14,12},{1,3},{3,1},... | collective-permute-start | bytes 688136 | tf_op jit(solution)/shard_map/ppermute | solution.py:329
  187.8 27.5 %collective-permute-start.11 = (bf16[128,1024]{1,0:T(8,128)(2,1)S(1)}, bf16[128,1024]{1,0:T(8,128)(2,1)S(1)}, u32[]{:S(2)}, u32[]{:S(2)}) collective-permute-start(bf16[128,1024]{1,0:T(8,128)(2,1)S(1)} %get-tuple-element.35), channel_id=1, source_target_pairs={{0,4},{2,6},{4,8},{6,10},{8,12},{10,14},{12,0},{14,2},{1,5},{3,7},... | collective-permute-start | bytes 786440 | tf_op jit(solution)/shard_map/ppermute | solution.py:291
  189.5 25.8 %collective-permute-start.12 = (bf16[128,1024]{1,0:T(8,128)(2,1)S(1)}, bf16[128,1024]{1,0:T(8,128)(2,1)S(1)}, u32[]{:S(2)}, u32[]{:S(2)}) collective-permute-start(bf16[128,1024]{1,0:T(8,128)(2,1)S(1)} %get-tuple-element.36), channel_id=1, source_target_pairs={{0,8},{2,10},{4,12},{6,14},{8,0},{10,2},{12,4},{14,6},{1,9},{3,11}... | collective-permute-start | bytes 786440 | tf_op jit(solution)/shard_map/ppermute | solution.py:291
  189.6 25.7 %collective-permute-start.13 = (bf16[128,1024]{1,0:T(8,128)(2,1)S(1)}, bf16[128,1024]{1,0:T(8,128)(2,1)S(1)}, u32[]{:S(2)}, u32[]{:S(2)}) collective-permute-start(bf16[128,1024]{1,0:T(8,128)(2,1)S(1)} %get-tuple-element.37), channel_id=1, source_target_pairs={{0,12},{2,14},{4,0},{6,2},{8,4},{10,6},{12,8},{14,10},{1,13},{3,15... | collective-permute-start | bytes 786440 | tf_op jit(solution)/shard_map/ppermute | solution.py:291
  198.1 30.4 %copy-start.5 = (bf16[5,128,1024]{2,1,0:T(8,128)(2,1)S(1)}, bf16[5,128,1024]{2,1,0:T(8,128)(2,1)}, u32[]{:S(2)}) copy-start(bf16[5,128,1024]{2,1,0:T(8,128)(2,1)} %copy-done.4) | copy-start | bytes 3932164
  198.1 16.0 %collective-permute-start.8 = (f32[56,1024]{1,0:T(8,128)S(1)}, f32[56,1024]{1,0:T(8,128)S(1)}, u32[]{:S(2)}, u32[]{:S(2)}) collective-permute-start(f32[56,1024]{1,0:T(8,128)S(1)} %add.243), channel_id=1, source_target_pairs={{0,4},{2,6},{4,0},{6,2},{8,12},{10,14},{12,8},{14,10},{1,5},{3,7},... | collective-permute-start | bytes 688136 | tf_op jit(solution)/shard_map/ppermute | solution.py:329
  214.1 12.4 %collective-permute-start.9 = (f32[56,1024]{1,0:T(8,128)S(1)}, f32[56,1024]{1,0:T(8,128)S(1)}, u32[]{:S(2)}, u32[]{:S(2)}) collective-permute-start(f32[56,1024]{1,0:T(8,128)S(1)} %add.244), channel_id=1, source_target_pairs={{0,8},{2,10},{4,12},{6,14},{8,0},{10,2},{12,4},{14,6},{1,9},{3,11}... | collective-permute-start | bytes 688136 | tf_op jit(solution)/shard_map/ppermute | solution.py:329
